TPU v7x, 128 devices: a whole 4x4x4 slice. The times are simulated.
128 devices in a mesh: dp: 8 (over y, x_hi), tx: 4 (over z), ty: 4 (over x_lo, core).
Axes of the slice: x: 4 (x_hi: 2, x_lo: 2; x = x_hi * 2 + x_lo), y: 4, z: 4, core: 2. Of those that a mesh axis runs over, the one named last changes fastest.
Arguments:
- tokens: bfloat16 [4096, 8192], P(('dp', 'tx', 'ty')), may hold values from -6 to 6
- mod_shift: bfloat16 [16, 8192], P('dp'), may hold values from -3 to 3
- mod_scale: bfloat16 [16, 8192], P('dp'), may hold values from -2.5 to 2.5
- up_weight: bfloat16 [8192, 16384], P(None, ('tx', 'ty')), may hold values from -0.0625 to 0.0625
- up_bias: bfloat16 [16384], P(('tx', 'ty')), may hold values from -4 to 4
- act_grad: bfloat16 [4096, 16384], P('dp', ('tx', 'ty')), may hold values from -24 to 24
Outputs:
- token_grad: bfloat16 [4096, 8192], P(('dp', 'tx', 'ty'))
- weight_grad: bfloat16 [8192, 16384], P('dp', ('tx', 'ty'))
- bias_grad: float32 [16384], P(('tx', 'ty'))
- shift_grad: float32 [16, 8192], P('dp')
- modulation_scale_gradient: float32 [16, 8192], P('dp')
All inputs are finite; a program needn't handle non-finite values.
Results may differ from a plain program's by a relative error of at most 0.029.
Values may be sent and summed in bfloat16 or wider, within the bound.
A program may use at most 256 MiB of HBM per device.

v0:
```python
import jax
import jax.numpy as jnp
from jax import lax
from jax.sharding import PartitionSpec as P


def layer_normalize(tokens):
    values = tokens.astype(jnp.float32)
    average = jnp.mean(values, axis=-1, keepdims=True)
    centered = values - average
    spread = jnp.mean(centered * centered, axis=-1, keepdims=True)
    inverse_deviation = lax.rsqrt(spread + 1e-06)
    return (centered * inverse_deviation, inverse_deviation)


def activation_grad(preact, act_grad):
    _, pullback = jax.vjp(lambda entries: jax.nn.gelu(entries, approximate=True), preact)
    return pullback(act_grad.astype(jnp.float32))[0]


def local(tokens, mod_shift, mod_scale, up_weight, up_bias, act_grad):
    local_rows = tokens.shape[0]
    width_of_model = tokens.shape[1]
    image_total = mod_shift.shape[0]
    group_rows = act_grad.shape[0]
    image_grouped = group_rows // image_total
    position = lax.axis_index(("tx", "ty"))
    collected_rows = lax.all_gather(tokens, ("tx", "ty"), axis=0, tiled=True)
    standardized_input, inverse_deviation = layer_normalize(collected_rows)
    scale_full = mod_scale.astype(jnp.float32)
    shift_full = mod_shift.astype(jnp.float32)
    reshaped_rows = standardized_input.reshape(image_total, image_grouped, width_of_model)
    normalized_rows = (
        (reshaped_rows * (1.0 + scale_full[:, None, :]) + shift_full[:, None, :])
        .reshape(group_rows, width_of_model)
        .astype(jnp.bfloat16)
    )
    preact = jnp.dot(
        normalized_rows, up_weight, preferred_element_type=jnp.float32
    ) + up_bias.astype(jnp.float32)
    grad_pre = activation_grad(preact, act_grad).astype(jnp.bfloat16)
    weight_grad = lax.psum_scatter(
        lax.dot_general(
            normalized_rows, grad_pre, (((0,), (0,)), ((), ())), preferred_element_type=jnp.float32
        ).astype(jnp.bfloat16),
        "dp",
        scatter_dimension=0,
        tiled=True,
    )
    bias_grad = lax.psum(jnp.sum(grad_pre.astype(jnp.float32), axis=0), "dp")
    leading_row = position * local_rows
    local_standardized = lax.dynamic_slice_in_dim(standardized_input, leading_row, local_rows, 0)
    own_inv = lax.dynamic_slice_in_dim(inverse_deviation, leading_row, local_rows, 0)
    sample_index = leading_row // image_grouped
    local_gradient = lax.psum_scatter(
        lax.dot_general(
            grad_pre, up_weight, (((1,), (1,)), ((), ())), preferred_element_type=jnp.float32
        ).astype(jnp.bfloat16),
        ("tx", "ty"),
        scatter_dimension=0,
        tiled=True,
    ).astype(jnp.float32)
    image_mask = (jnp.arange(image_total) == sample_index).astype(jnp.float32)[:, None]
    shift_term = image_mask * jnp.sum(local_gradient, axis=0)[None, :]
    scale_contribution = image_mask * jnp.sum(local_gradient * local_standardized, axis=0)[None, :]
    shift_grad, modulation_scale_gradient = (
        lax.psum(shift_term.astype(jnp.bfloat16), ("tx", "ty")).astype(jnp.float32),
        lax.psum(scale_contribution.astype(jnp.bfloat16), ("tx", "ty")).astype(jnp.float32),
    )
    own_scale = lax.dynamic_slice_in_dim(scale_full, sample_index, 1, 0)
    gradient_scaled = local_gradient * (1.0 + own_scale)
    gradient_centered = (
        gradient_scaled
        - jnp.mean(gradient_scaled, axis=-1, keepdims=True)
        - local_standardized
        * jnp.mean(gradient_scaled * local_standardized, axis=-1, keepdims=True)
    )
    token_grad = (own_inv * gradient_centered).astype(jnp.bfloat16)
    return (token_grad, weight_grad, bias_grad, shift_grad, modulation_scale_gradient)


def solution(mesh):
    return jax.shard_map(
        local,
        mesh=mesh,
        in_specs=(
            P(("dp", "tx", "ty"), None),
            P("dp", None),
            P("dp", None),
            P(None, ("tx", "ty")),
            P(("tx", "ty")),
            P("dp", ("tx", "ty")),
        ),
        out_specs=(
            P(("dp", "tx", "ty"), None),
            P("dp", ("tx", "ty")),
            P(("tx", "ty")),
            P("dp", None),
            P("dp", None),
        ),
        check_vma=False,
    )
```

profile of v0, /device:TPU:0, one launch (start us, length us, event | category | flops | bytes accessed | tf_op | source)
XLA Modules:
  0.0 529.4 jit_solution(16901184558584052081)
XLA Ops:
  7.2 0.0 all-gather.2.cloned.1.call-start
  7.2 0.7 all-gather.2.cloned.1.call-update
  7.9 0.0 reduce-scatter.3.cloned.1.call-start
  7.9 0.7 convert_element_type.60
  8.6 0.8 convert_element_type.58
  9.4 0.8 broadcast_add_fusion
  10.2 54.2 %all-gather.2.cloned.1.call-done = bf16[512,8192]{1,0:T(8,128)(2,1)} async-done(((bf16[32,8192]{1,0:T(8,128)(2,1)}), bf16[512,8192]{1,0:T(8,128)(2,1)}) %all-gather.2.cloned.1.call-update) | async-done | bytes 8388624 | tf_op jit(solution)/shard_map/all_gather | solution.py:28
  64.4 4.7 convert_reduce_fusion
  69.1 1.0 copy-done
  70.1 2.3 fusion.2
  72.5 0.0 copy-start.4
  72.5 7.1 %fusion = (f32[512,8192]{1,0:T(8,128)}, bf16[512,8192]{1,0:T(8,128)(2,1)S(1)}) fusion(bf16[512,8192]{1,0:T(8,128)(2,1)S(1)} %copy-done, f32[512]{0:T(512)S(1)} %add_rsqrt_fusion, f32[512]{0:T(512)S(1)} %broadcast_multiply_fusion, f32[2,8192]{1,0:T(2,128)S(1)} %convert_element_type.58, f32[2,8192]{1,0:T(2,128)S(1)} %broadcast_add_fusion), kind=kLoop, calls=%fused_computation.2 | loop fusion | flops 25165824 | bytes 33689600 | tf_op jit(solution)/shard_map/mul | solution.py:13
  79.6 0.0 copy-done.4
  79.6 16.9 %convert_reduce_fusion.1 = (f32[1024]{0:T(1024)S(1)}, f32[512,1024]{1,0:T(8,128)S(1)}) fusion(bf16[512,1024]{1,0:T(8,128)(2,1)S(1)} %copy-done.4, f32[1024]{0:T(1024)S(1)} %convert_element_type.60, bf16[512,8192]{1,0:T(8,128)(2,1)S(1)} %get-tuple-element.12, bf16[8192,1024]{1,0:T(8,128)(2,1)} %param.9), kind=kOutput, calls=%fused_computation.24 | convolution fusion | flops 8602516480 | bytes 28319744 | tf_op jit(solution)/shard_map/dot_general | solution.py:38
  96.5 25.2 %convolution_convert_fusion.1 = bf16[512,8192]{1,0:T(8,128)(2,1)} fusion(bf16[8192,1024]{1,0:T(8,128)(2,1)} %param.9, bf16[512,1024]{1,0:T(8,128)(2,1)S(1)} %copy-done.4, f32[512,1024]{1,0:T(8,128)S(1)} %get-tuple-element.16, f32[1024]{0:T(1024)S(1)} %convert_element_type.60), kind=kOutput, calls=%fused_computation.9 | convolution fusion | flops 8605663232 | bytes 28315648 | tf_op jit(solution)/shard_map/dot_general | solution.py:56
  121.7 0.0 reduce-scatter.3.cloned.1.call-update
  121.7 0.2 all-reduce.3.cloned.1.call-start
  121.9 0.5 copy-done.3
  122.5 98.3 %reduce-scatter.3.cloned.1.call-done = bf16[32,8192]{1,0:T(8,128)(2,1)} async-done(((bf16[512,8192]{1,0:T(8,128)(2,1)}), bf16[32,8192]{1,0:T(8,128)(2,1)}) %reduce-scatter.3.cloned.1.call-update) | async-done | bytes 524304 | tf_op jit(solution)/shard_map/reduce_scatter | solution.py:55
  220.8 1.9 fusion.23
  222.7 0.7 multiply_convert_fusion
  223.4 0.0 all-reduce.3.cloned.1.call-update
  223.5 0.0 reduce-scatter.5.cloned.1.call-start
  223.5 16.6 %convolution_convert_fusion = bf16[8192,1024]{1,0:T(8,128)(2,1)} fusion(bf16[512,8192]{1,0:T(8,128)(2,1)} %copy-done.1, bf16[512,1024]{1,0:T(8,128)(2,1)S(1)} %copy-done.4, f32[512,1024]{1,0:T(8,128)S(1)} %get-tuple-element.16, f32[1024]{0:T(1024)S(1)} %convert_element_type.60), kind=kOutput, calls=%fused_computation.8 | convolution fusion | flops 8609857536 | bytes 28315648 | tf_op jit(solution)/shard_map/dot_general | solution.py:43
  240.2 0.0 reduce-scatter.5.cloned.1.call-update
  240.2 0.1 dynamic-slice.3
  240.3 24.6 %psum.21 = f32[1024]{0:T(1024)} all-reduce(f32[1024]{0:T(1024)S(1)} %get-tuple-element.15), channel_id=1, replica_groups=mesh['dp'=8,'tx'=4,'ty'=4] {'dp'}, use_global_device_ids=true, to_apply=%region_7.8 | all-reduce | flops 1024 | bytes 8192 | tf_op jit(solution)/shard_map/psum | solution.py:50
  264.9 2.3 fusion.21
  267.2 61.0 %all-reduce.3.cloned.1.call-done = (bf16[2,8192]{1,0:T(2,128)(2,1)}, bf16[2,8192]{1,0:T(2,128)(2,1)}) async-done(((bf16[2,8192]{1,0:T(2,128)(2,1)}, bf16[2,8192]{1,0:T(2,128)(2,1)}), (bf16[2,8192]{1,0:T(2,128)(2,1)}, bf16[2,8192]{1,0:T(2,128)(2,1)})) %all-reduce.3.cloned.1.call-update) | async-done | bytes 65552 | tf_op jit(solution)/shard_map/psum | solution.py:67
  328.2 1.4 convert_element_type.69
  329.6 1.4 convert_element_type.71
  331.0 191.9 %reduce-scatter.5.cloned.1.call-done = bf16[1024,1024]{1,0:T(8,128)(2,1)} async-done(((bf16[8192,1024]{1,0:T(8,128)(2,1)}), bf16[1024,1024]{1,0:T(8,128)(2,1)}) %reduce-scatter.5.cloned.1.call-update) | async-done | bytes 2097168 | tf_op jit(solution)/shard_map/reduce_scatter | solution.py:42
  (12 shorter events, 0.1 us)
Async XLA Ops:
  7.2 57.2 %all-gather.2.cloned.1.call-start = ((), (), s32[]{:S(2)}) async-start(), calls=%async_computation.2 | async-start | bytes 8912896 | tf_op jit(solution)/shard_map/all_gather | solution.py:28
  7.9 212.9 %reduce-scatter.3.cloned.1.call-start = ((), (), s32[]{:S(2)}) async-start(), calls=%async_computation.3 | async-start | bytes 8912896 | tf_op jit(solution)/shard_map/reduce_scatter | solution.py:55
  64.4 5.8 %copy-start = (bf16[512,8192]{1,0:T(8,128)(2,1)S(1)}, bf16[512,8192]{1,0:T(8,128)(2,1)}, u32[]{:S(2)}) copy-start(bf16[512,8192]{1,0:T(8,128)(2,1)} %all-gather.2.cloned.1.call-done) | copy-start | bytes 25165828
  72.5 7.1 %copy-start.4 = (bf16[512,1024]{1,0:T(8,128)(2,1)S(1)}, bf16[512,1024]{1,0:T(8,128)(2,1)}, u32[]{:S(2)}) copy-start(bf16[512,1024]{1,0:T(8,128)(2,1)} %param.11) | copy-start | bytes 3145732
  79.6 16.9 %copy-start.1 = (bf16[512,8192]{1,0:T(8,128)(2,1)}, bf16[512,8192]{1,0:T(8,128)(2,1)S(1)}, u32[]{:S(2)}) copy-start(bf16[512,8192]{1,0:T(8,128)(2,1)S(1)} %get-tuple-element.12) | copy-start | bytes 25165828
  121.7 0.8 copy-start.3
  121.7 206.5 %all-reduce.3.cloned.1.call-start = ((), (), s32[]{:S(2)}) async-start(), calls=%async_computation.5 | async-start | bytes 131072 | tf_op jit(solution)/shard_map/psum | solution.py:67
  223.5 299.4 %reduce-scatter.5.cloned.1.call-start = ((), (), s32[]{:S(2)}) async-start(), calls=%async_computation.4 | async-start | bytes 18874368 | tf_op jit(solution)/shard_map/reduce_scatter | solution.py:42
  240.2 24.7 %copy-start.2 = (bf16[32,8192]{1,0:T(8,128)(2,1)S(1)}, bf16[32,8192]{1,0:T(8,128)(2,1)}, u32[]{:S(2)}) copy-start(bf16[32,8192]{1,0:T(8,128)(2,1)} %reduce-scatter.3.cloned.1.call-done) | copy-start | bytes 1572868
Sparse Core Ops, SparseCore 0:
  9.7 54.6 all-gather.1
  121.8 98.9 reduce-scatter.2
  223.9 104.2 all-reduce.2
  333.1 189.7 reduce-scatter.4
where the time goes:
time: 530 us; the launch traced here: 529 us
  waiting for transfers between devices  406 us (77%)
  matrix products  58.7 us (11%)
  blocking collectives  24.6 us (5%)
  other arithmetic  24.2 us (5%)
  between operations  13.8 us (3%)
    reduce_scatter x1, waiting for transfers between devices, local(): lax.psum_scatter(lax.dot_general(normalized_rows, grad_pre, (((0,), (0,))...  192 us
    reduce_scatter x1, waiting for transfers between devices, local(): lax.psum_scatter(lax.dot_general(grad_pre, up_weight, (((1,), (1,)), ((),...  98.3 us
    psum x1, waiting for transfers between devices, local(): lax.psum(shift_term.astype(jnp.bfloat16), ('tx', 'ty')).astype(jnp.float32)  61 us
    all_gather x1, waiting for transfers between devices, local(): collected_rows = lax.all_gather(tokens, ('tx', 'ty'), axis=0, tiled=True)  54.2 us
    dot_general x1, matrix products, local(): lax.dot_general(grad_pre, up_weight, (((1,), (1,)), ((), ())), preferred_...  25.2 us
    psum x1, blocking collectives, local(): bias_grad = lax.psum(jnp.sum(grad_pre.astype(jnp.float32), axis=0), 'dp')  24.6 us
    dot_general x1, matrix products, local(): jnp.dot(normalized_rows, up_weight, preferred_element_type=jnp.float32)  16.9 us
    dot_general x1, matrix products, local(): lax.dot_general(normalized_rows, grad_pre, (((0,), (0,)), ((), ())), pref...  16.6 us
  transfers between devices with their start and end apart: 4, of which 4 were waited for; matrix products, arithmetic and copies ran while one was open for 5% of the time, Pallas kernels for 0%

commit v1 on v0

v1 whole, which is shorter than its diff:
```python
import functools

import jax
import jax.numpy as jnp
from jax import lax
from jax.experimental import pallas as pl
from jax.experimental.pallas import tpu as pltpu
from jax.sharding import PartitionSpec as P

MESH = pl.DeviceIdType.MESH
MIB = 1 << 20
F32 = jnp.float32
BF16 = jnp.bfloat16
GELU_A = 0.7978845608028654
GELU_B = 0.044715


def place():
    dp, tx, ty = (lax.axis_index(a) for a in ("dp", "tx", "ty"))
    return dp // 2, dp % 2, tx, ty // 2, ty % 2


def peer(dy=0, dh=0, dz=0, dl=0, dc=0):
    y, h, z, l, c = place()
    return (
        lax.rem(y + dy, 4) * 2 + lax.rem(h + dh, 2),
        lax.rem(z + dz, 4),
        lax.rem(l + dl, 2) * 2 + lax.rem(c + dc, 2),
    )


def greet(peers):
    barrier = pltpu.get_barrier_semaphore()
    for p in peers:
        pl.semaphore_signal(barrier, inc=1, device_id=p, device_id_type=MESH)
    pl.semaphore_wait(barrier, len(peers))


def remote(src, dst, send, recv, to):
    return pltpu.make_async_remote_copy(
        src_ref=src, dst_ref=dst, send_sem=send, recv_sem=recv, device_id=to, device_id_type=MESH
    )


def landed(ref, sem):
    pltpu.make_async_copy(ref, ref, sem).wait()


def cols(i, n):
    return pl.ds(pl.multiple_of(i * n, n), n)


def standardize(tok_ref):
    values = tok_ref[...].astype(F32)
    average = jnp.mean(values, axis=-1, keepdims=True)
    centered = values - average
    spread = jnp.mean(centered * centered, axis=-1, keepdims=True)
    inv = lax.rsqrt(spread + 1e-06)
    return centered * inv, inv


def own_image(ref):
    _, _, z, _, _ = place()
    m = ref[...].astype(F32)
    first = (z < 2).astype(F32)
    return jnp.where(first > 0.5, m[0:1], m[1:2])


def slot(c, z, l):
    return c * 8 + z * 2 + l


def rows(c, z, l):
    return pl.ds(slot(c, z, l) * 32, 32)


PIECES = ((0, 0), (0, 1), (3, 0), (1, 0), (3, 1), (1, 1), (2, 0), (2, 1))


def gather_kernel(
    tok, shift, scale, w_hbm, bias, act, g_out, gt_out, cb,
    n, w, w_sem, n_send, n_recv, c_send, c_recv, f_send, f_recv, o_sem,
):
    y, _, z, l, c = place()
    sib = peer(dc=1)
    pair = peer(dl=1)
    ring = {d: peer(dz=d) for d in (1, 2, 3)}
    group = {d: peer(dy=d) for d in (1, 2, 3)}

    load_w = pltpu.make_async_copy(w_hbm, w, w_sem)
    load_w.start()
    greet([sib, pair, *ring.values(), *group.values()])

    xhat, _ = standardize(tok)
    n[rows(0, 0, 0), :] = (xhat * (1.0 + own_image(scale)) + own_image(shift)).astype(BF16)

    pending = []

    def send(src, dst, to):
        s, d = rows(*src), rows(*dst)
        cp = remote(n.at[s], n.at[d], n_send.at[len(pending)], n_recv.at[slot(*dst)], to)
        cp.start()
        pending.append(cp)

    def exchange(zz, ll):
        p = zz * 2 + ll
        for d in (2, 1, 3):
            block = lax.rem(y + d, 4)
            src = n.at[rows(0, zz, ll), cols(block, 2048)]
            cp = remote(
                src, cb.at[4 - d, rows(0, zz, ll)], c_send.at[d - 1, p], c_recv.at[3 - d, p], group[d]
            )
            cp.start()

    def arrived(*s):
        landed(n.at[rows(*s)], n_recv.at[slot(*s)])

    def block(zz):
        for ll in (0, 1):
            arrived(1, zz, ll)
        a, b = zz * 64, 256 + zz * 64
        at = []
        for cc in (0, 1):
            for ll in (0, 1):
                zr = lax.rem(z + zz, 4)
                at.append((zr * 4 + lax.rem(l + ll, 2) * 2 + lax.rem(c + cc, 2)) * 32)

        @pl.loop(0, 4)
        def _(j):
            t = cols(j, 256)
            x = jnp.concatenate([n[a : a + 64, :], n[b : b + 64, :]], axis=0)
            pre = jnp.dot(x, w[:, t], preferred_element_type=F32) + bias[:, t].astype(F32)
            up = jnp.concatenate([act[pl.ds(pl.multiple_of(r, 32), 32), t] for r in at], axis=0).astype(F32)
            sq = pre * pre
            th = jnp.tanh(GELU_A * pre * (1.0 + GELU_B * sq))
            slope = 0.5 * (1.0 + th) + 0.5 * GELU_A * pre * (1.0 - th * th) * (1.0 + 3.0 * GELU_B * sq)
            grad = (up * slope).astype(BF16)
            g_out[a : a + 64, t] = grad[0:64]
            g_out[b : b + 64, t] = grad[64:128]

    own = (0, 0, 0)
    send(own, (0, 0, 1), pair)
    for d in (1, 3, 2):
        send(own, (0, 4 - d, 0), ring[d])
    send(own, (1, 0, 0), sib)
    exchange(0, 0)

    arrived(0, 0, 1)
    for d in (1, 3, 2):
        send((0, 0, 1), (0, 4 - d, 1), ring[d])
    send((0, 0, 1), (1, 0, 1), sib)
    exchange(0, 1)
    load_w.wait()
    block(0)
    for zz, ll in ((3, 0), (1, 0), (3, 1), (1, 1)):
        arrived(0, zz, ll)
        send((0, zz, ll), (1, zz, ll), sib)
        exchange(zz, ll)
    block(3)
    block(1)
    for ll in (0, 1):
        arrived(0, 2, ll)
        send((0, 2, ll), (1, 2, ll), sib)
        exchange(2, ll)
    block(2)

    keep = pltpu.make_async_copy(n.at[:, cols(y, 2048)], cb.at[0], o_sem)
    keep.start()

    @pl.loop(0, 4)
    def _(j):
        gt_out[cols(j, 256), :] = g_out[:, cols(j, 256)].T

    moved = []
    for zz, ll in PIECES:
        p = zz * 2 + ll
        for s in (1, 2, 3):
            src = cb.at[s, rows(0, zz, ll)]
            landed(src, c_recv.at[s - 1, p])
            cp = remote(src, cb.at[s, rows(1, zz, ll)], f_send.at[s - 1, p], f_recv.at[s - 1, p], sib)
            cp.start()
            moved.append(cp)
    for cp in moved:
        cp.wait()
    for cp in pending:
        cp.wait_send()
    for zz, ll in PIECES:
        for s in (0, 1, 2):
            src = n.at[rows(0, zz, ll), pl.ds(0, 2048)]
            landed(src, c_send.at[s, zz * 2 + ll])
    keep.wait()


NF = 8
ND = 8


def grad_kernel(
    tok, scale, g, gt, cb_hbm, w_hbm, token_grad, weight_grad, bias_grad, shift_grad, scale_grad,
    w, cb, gb, sb, rb, zs, zr, xs, xr, keep, xhat, inv, part, pws, xw, bsum, brec, term, trec,
    w_sem, cb_sem, y_send, y_recv, s_send, s_recv, z_send, z_recv, l_send, l_recv, x_send, x_recv,
    b_send, b_recv, t_send, t_recv,
):
    _, h, z, _, _ = place()
    sib = peer(dc=1)
    pair = peer(dl=1)
    ring = {d: peer(dz=d) for d in (1, 2, 3)}
    group = {d: peer(dy=d) for d in (1, 2, 3)}
    cross = peer(dh=1)
    fc, dc = 1024 // NF, 8192 // ND

    load_w = pltpu.make_async_copy(w_hbm, w, w_sem)
    load_w.start()
    load_cb = pltpu.make_async_copy(cb_hbm, cb, cb_sem)
    load_cb.start()
    greet([sib, pair, *ring.values(), *group.values(), cross])

    def y_copy(d, q):
        return remote(
            gt.at[cols(q, fc)], gb.at[3 - d, cols(q, fc)], y_send.at[d - 1, q], y_recv.at[3 - d, q], group[d]
        )

    @pl.loop(0, NF)
    def _(q):
        for d in (2, 1, 3):
            y_copy(d, q).start()

    xh, iv = standardize(tok)
    xhat[...] = xh
    inv[...] = jnp.broadcast_to(iv, inv.shape)
    load_w.wait()

    def s_copy(j):
        k = lax.rem(j, 2)
        return remote(sb.at[k], rb.at[:, cols(j, dc)], s_send.at[k], s_recv.at[j], sib)

    def z_copy(d, j):
        return remote(
            zs.at[pl.ds(d * 64, 64), cols(j, dc)],
            zr.at[3 - d, :, cols(j, dc)],
            z_send.at[d - 1, j],
            z_recv.at[3 - d, j],
            ring[d],
        )

    def core_sum(j):
        t = cols(j, dc)
        landed(rb.at[:, t], s_recv.at[j])
        zs[:, t] = (zs[:, t].astype(F32) + rb[:, t].astype(F32)).astype(BF16)
        for d in (2, 1, 3):
            z_copy(d, j).start()

    @pl.loop(0, ND)
    def _(j):
        k = lax.rem(j, 2)

        @pl.when(j >= 2)
        def _():
            s_copy(j).wait_send()

        @pl.loop(0, dc // 512)
        def _(i):
            t = pl.ds(pl.multiple_of(j * dc + i * 512, 512), 512)
            p = lax.dot_general(g[...], w[t, :], (((1,), (1,)), ((), ())), preferred_element_type=F32)
            p = p.astype(BF16)
            zs[:, t] = p[0:256]
            sb[k, :, cols(i, 512)] = p[256:512]

        s_copy(j).start()

        @pl.when(j >= 1)
        def _():
            core_sum(j - 1)

    core_sum(ND - 1)
    s_copy(0).wait_send()
    s_copy(1).wait_send()
    load_cb.wait()

    def x_copy(q):
        return remote(pws.at[cols(q, fc)], xw.at[cols(q, fc)], x_send.at[q], x_recv.at[q], cross)

    def l_copy(j):
        return remote(xs.at[:, cols(j, dc)], xr.at[:, cols(j, dc)], l_send.at[j], l_recv.at[j], pair)

    def weight_part(q):
        r = cols(q, fc)
        for s in range(3):
            landed(gb.at[s, r], y_recv.at[s, q])

        def tile(column):
            t = pl.ds(pl.multiple_of(column, 512), 512)
            acc = jnp.dot(gt[r, :], cb[0, :, t], preferred_element_type=F32)
            for s in range(3):
                acc += jnp.dot(gb[s, r, :], cb[s + 1, :, t], preferred_element_type=F32)
            return acc

        @pl.loop(0, 2)
        def _(i):
            pws[r, cols(i, 512)] = tile((1 - h) * 1024 + i * 512).astype(BF16)

        x_copy(q).start()

        @pl.loop(0, 2)
        def _(i):
            part[r, cols(i, 512)] = tile(h * 1024 + i * 512)

        ones = jnp.ones((8, 512), BF16)
        nt = (((1,), (1,)), ((), ()))
        total = lax.dot_general(ones, gt[r, :], nt, preferred_element_type=F32)
        for s in range(3):
            total += lax.dot_general(ones, gb[s, r, :], nt, preferred_element_type=F32)
        bsum[:, r] = total

    def weight_sum(q):
        r = cols(q, fc)
        landed(xw.at[r], x_recv.at[q])
        weight_grad[:, r] = (part[r, :] + xw[r, :].astype(F32)).T.astype(BF16)

    def z_sum(j):
        t = cols(j, dc)
        for s in range(3):
            landed(zr.at[s, :, t], z_recv.at[s, j])
        total = zs[0:64, t].astype(F32)
        for s in range(3):
            total += zr[s, :, t].astype(F32)
        keep[:, t] = total[0:32]
        xs[:, t] = total[32:64].astype(BF16)
        l_copy(j).start()

    def row_sum(j):
        t = cols(j, dc)
        landed(xr.at[:, t], l_recv.at[j])
        own = keep[:, t] + xr[:, t].astype(F32)
        keep[:, t] = own
        term[0, 0:1, t] = jnp.sum(own, axis=0, keepdims=True)
        term[0, 1:2, t] = jnp.sum(own * xhat[:, t], axis=0, keepdims=True)

    @pl.loop(0, NF)
    def _(q):
        weight_part(q)
        z_sum(q)

        @pl.when(q >= 1)
        def _():
            row_sum(q - 1)

        @pl.when(q >= 4)
        def _():
            weight_sum(q - 4)

    b_copy = remote(bsum, brec, b_send.at[0], b_recv.at[0], cross)
    b_copy.start()
    row_sum(ND - 1)

    flip = lax.rem(z, 2)
    near = (peer()[0], z + 1 - 2 * flip, peer()[2])

    def t_copy(k, to):
        return remote(term.at[k], trec.at[k], t_send.at[k], t_recv.at[k], to)

    partners = (sib, pair, near, ring[2])
    hops = [t_copy(k, to) for k, to in enumerate(partners)]
    hops[0].start()

    grown = 1.0 + own_image(scale)
    scaled = keep[...] * grown
    mean_one = jnp.mean(scaled, axis=-1, keepdims=True)
    mean_two = jnp.mean(scaled * xhat[...], axis=-1, keepdims=True)
    token_grad[...] = (inv[:, 0:1] * (scaled - mean_one - xhat[...] * mean_two)).astype(BF16)

    for k in range(3):
        hops[k].wait_recv()
        term[k + 1] = term[k] + trec[k]
        hops[k + 1].start()
        weight_sum(NF - 4 + k)
    b_copy.wait()
    bias_grad[...] = bsum[...] + brec[...]
    hops[3].wait_recv()
    first = (z < 2).astype(F32) > 0.5
    mine, other = term[3], trec[3]
    shift_grad[0:1, :] = jnp.where(first, mine[0:1], other[0:1])
    shift_grad[1:2, :] = jnp.where(first, other[0:1], mine[0:1])
    scale_grad[0:1, :] = jnp.where(first, mine[1:2], other[1:2])
    scale_grad[1:2, :] = jnp.where(first, other[1:2], mine[1:2])
    weight_sum(NF - 1)

    for k in range(4):
        hops[k].wait_send()

    @pl.loop(0, NF)
    def _(q):
        for d in (1, 2, 3):
            y_copy(d, q).wait_send()
            z_copy(d, q).wait_send()
        l_copy(q).wait_send()
        x_copy(q).wait_send()


def local(tokens, mod_shift, mod_scale, up_weight, up_bias, act_grad):
    vmem = pl.BlockSpec(memory_space=pltpu.VMEM)
    hbm = pl.BlockSpec(memory_space=pltpu.HBM)
    dma = pltpu.SemaphoreType.DMA
    g, gt, cb = pl.pallas_call(
        gather_kernel,
        out_shape=(
            jax.ShapeDtypeStruct((512, 1024), BF16),
            jax.ShapeDtypeStruct((1024, 512), BF16),
            jax.ShapeDtypeStruct((4, 512, 2048), BF16),
        ),
        in_specs=[vmem, vmem, vmem, hbm, vmem, vmem],
        out_specs=(vmem, vmem, hbm),
        scratch_shapes=[
            pltpu.VMEM((512, 8192), BF16),
            pltpu.VMEM((8192, 1024), BF16),
            dma(()),
            dma((15,)),
            dma((16,)),
            dma((3, 8)),
            dma((3, 8)),
            dma((3, 8)),
            dma((3, 8)),
            dma(()),
        ],
        compiler_params=pltpu.CompilerParams(
            collective_id=0, has_side_effects=True, vmem_limit_bytes=48 * MIB
        ),
        name="gather_up",
    )(tokens, mod_shift, mod_scale, up_weight, up_bias[None, :], act_grad)
    token_grad, weight_grad, bias_grad, shift_grad, scale_grad = pl.pallas_call(
        grad_kernel,
        out_shape=(
            jax.ShapeDtypeStruct((32, 8192), BF16),
            jax.ShapeDtypeStruct((1024, 1024), BF16),
            jax.ShapeDtypeStruct((8, 1024), F32),
            jax.ShapeDtypeStruct((2, 8192), F32),
            jax.ShapeDtypeStruct((2, 8192), F32),
        ),
        in_specs=[vmem, vmem, vmem, vmem, hbm, hbm],
        out_specs=(vmem,) * 5,
        scratch_shapes=[
            pltpu.VMEM((8192, 1024), BF16),
            pltpu.VMEM((4, 512, 2048), BF16),
            pltpu.VMEM((3, 1024, 512), BF16),
            pltpu.VMEM((2, 256, 8192 // ND), BF16),
            pltpu.VMEM((256, 8192), BF16),
            pltpu.VMEM((256, 8192), BF16),
            pltpu.VMEM((3, 64, 8192), BF16),
            pltpu.VMEM((32, 8192), BF16),
            pltpu.VMEM((32, 8192), BF16),
            pltpu.VMEM((32, 8192), F32),
            pltpu.VMEM((32, 8192), F32),
            pltpu.VMEM((32, 128), F32),
            pltpu.VMEM((1024, 1024), F32),
            pltpu.VMEM((1024, 1024), BF16),
            pltpu.VMEM((1024, 1024), BF16),
            pltpu.VMEM((8, 1024), F32),
            pltpu.VMEM((8, 1024), F32),
            pltpu.VMEM((4, 2, 8192), F32),
            pltpu.VMEM((4, 2, 8192), F32),
            dma(()),
            dma(()),
            dma((3, NF)),
            dma((3, NF)),
            dma((2,)),
            dma((ND,)),
            dma((3, ND)),
            dma((3, ND)),
            dma((ND,)),
            dma((ND,)),
            dma((NF,)),
            dma((NF,)),
            dma((1,)),
            dma((1,)),
            dma((4,)),
            dma((4,)),
        ],
        compiler_params=pltpu.CompilerParams(
            collective_id=1, has_side_effects=True, vmem_limit_bytes=60 * MIB
        ),
        name="grads",
    )(tokens, mod_scale, g, gt, cb, up_weight)
    return token_grad, weight_grad, bias_grad[0], shift_grad, scale_grad


def solution(mesh):
    return jax.shard_map(
        local,
        mesh=mesh,
        in_specs=(
            P(("dp", "tx", "ty"), None),
            P("dp", None),
            P("dp", None),
            P(None, ("tx", "ty")),
            P(("tx", "ty")),
            P("dp", ("tx", "ty")),
        ),
        out_specs=(
            P(("dp", "tx", "ty"), None),
            P("dp", ("tx", "ty")),
            P(("tx", "ty")),
            P("dp", None),
            P("dp", None),
        ),
        check_vma=False,
    )
```

time: 530 us -> 193 us (0.36)
  waiting for transfers between devices: 406 us -> 0 us
  Pallas kernels: 0 us -> 174 us
  matrix products: 58.7 us -> 0 us
  blocking collectives: 24.6 us -> 0 us
  other arithmetic: 24.2 us -> 0 us
  local copies, waits for them, and re-layouts: 1.63 us -> 15.7 us
  between operations: 13.8 us -> 0.66 us
    reduce_scatter x2 -> x0, waiting for transfers between devices: 290 us -> none  [the longest x1 192 us: local(): lax.psum_scatter(lax.dot_general(normalized_rows, grad_pre, (((0,), (0,))...]
    pallas_call x0 -> x2, Pallas kernels: none -> 174 us  [the longest x1 93.6 us: local(): pl.pallas_call(grad_kernel, out_shape=(jax.ShapeDtypeStruct((32, 8192), B...]
    psum x1 -> x0, waiting for transfers between devices: 61 us -> none  [local(): lax.psum(shift_term.astype(jnp.bfloat16), ('tx', 'ty')).astype(jnp.float32)]
    dot_general x3 -> x0, matrix products: 58.7 us -> none  [the longest x1 25.2 us: local(): lax.dot_general(grad_pre, up_weight, (((1,), (1,)), ((), ())), preferred_...]
    all_gather x1 -> x0, waiting for transfers between devices: 54.2 us -> none  [local(): collected_rows = lax.all_gather(tokens, ('tx', 'ty'), axis=0, tiled=True)]
    psum x1 -> x0, blocking collectives: 24.6 us -> none  [local(): bias_grad = lax.psum(jnp.sum(grad_pre.astype(jnp.float32), axis=0), 'dp')]
    unnamed x10 -> x16, local copies, waits for them, and re-layouts: 1.55 us -> 13.6 us
    reduce_sum x3 -> x0, other arithmetic: 8.92 us -> none  [the longest x1 4.72 us: layer_normalize(): average = jnp.mean(values, axis=-1, keepdims=True)]
  transfers between devices with their start and end apart: 4 -> 0, of which waited for: 4 -> 0; matrix products, arithmetic and copies ran while one was open for 5% -> 0% of each run, Pallas kernels for 0% -> 0%
where the time goes in v1:
time: 193 us; the launch traced here: 191 us
  Pallas kernels  174 us (90%)
  local copies, waits for them, and re-layouts  15.7 us (8%)
    pallas_call x1, Pallas kernels, local(): pl.pallas_call(grad_kernel, out_shape=(jax.ShapeDtypeStruct((32, 8192), B...  93.6 us
    pallas_call x1, Pallas kernels, local(): pl.pallas_call(gather_kernel, out_shape=(jax.ShapeDtypeStruct((512, 1024)...  80.6 us
    unnamed x16, local copies, waits for them, and re-layouts  13.6 us

profile of v1, /device:TPU:0, one launch (start us, length us, event | category | flops | bytes accessed | tf_op | source)
XLA Modules:
  0.0 190.6 jit_solution(10593673529599790113)
XLA Ops:
  0.6 0.7 broadcast_in_dim.3.bias
  1.3 0.0 copy-start
  1.3 1.0 copy-done
  2.4 0.0 copy-start.1
  2.4 1.2 copy-done.1
  3.6 0.0 copy-start.4
  3.6 0.8 copy-done.4
  4.3 0.0 copy-start.5
  4.3 0.8 copy-done.5
  5.1 80.6 %gather_up.1 = (bf16[512,1024]{1,0:T(8,128)(2,1)S(1)}, bf16[1024,512]{1,0:T(8,128)(2,1)S(1)}, bf16[4,512,2048]{2,1,0:T(8,128)(2,1)}) custom-call(bf16[32,8192]{1,0:T(8,128)(2,1)S(1)} %copy-done, bf16[2,8192]{1,0:T(2,128)(2,1)S(1)} %copy-done.5, bf16[2,8192]{1,0:T(2,128)(2,1)S(1)} %copy-done.4, bf16[8192,1024]{1,0:T(8,128)(2,1)} %w_hbm.3, ...), custom_call_target="tpu_custom_call" | custom-call | tf_op jit(solution)/shard_map/gather_up/pallas_call | solution.py:404
  85.7 0.0 copy-start.2
  85.8 1.0 copy-done.2
  86.7 0.0 copy-start.3
  86.7 1.0 copy-done.3
  87.7 93.6 %grads.1 = (bf16[32,8192]{1,0:T(8,128)(2,1)}, bf16[1024,1024]{1,0:T(8,128)(2,1)}, f32[8,1024]{1,0:T(8,128)}, f32[2,8192]{1,0:T(2,128)}, f32[2,8192]{1,0:T(2,128)}) custom-call(bf16[32,8192]{1,0:T(8,128)(2,1)} %tok.3, bf16[2,8192]{1,0:T(2,128)(2,1)} %scale.3, bf16[512,1024]{1,0:T(8,128)(2,1)} %copy-done.2, bf16[1024,512]{1,0:T(8,128)(2,1)} %copy-done.3, ...), custom_call_target="tpu_custom_call" | custom-call | tf_op jit(solution)/shard_map/grads/pallas_call | solution.py:430
  181.3 1.4 slice.3
  182.7 1.9 copy.15
  184.5 3.1 %copy.16 = bf16[1024,1024]{1,0:T(8,128)(2,1)} copy(bf16[1024,1024]{1,0:T(8,128)(2,1)} %get-tuple-element.27) | data formatting | bytes 4194304
  187.6 1.5 copy.17
  189.1 1.5 copy.18
Async XLA Ops:
  1.3 1.0 copy-start
  2.4 1.2 copy-start.1
  3.6 0.8 copy-start.4
  4.3 0.8 copy-start.5
  85.7 1.0 copy-start.2
  86.7 1.0 copy-start.3

commit v2 on v1

v2 whole, which is shorter than its diff:
```python
import jax
import jax.numpy as jnp
from jax import lax
from jax.experimental import pallas as pl
from jax.experimental.pallas import tpu as pltpu
from jax.sharding import PartitionSpec as P

MESH = pl.DeviceIdType.MESH
MIB = 1 << 20
F32 = jnp.float32
BF16 = jnp.bfloat16
GELU_A = 0.7978845608028654
GELU_B = 0.044715


def place():
    dp, tx, ty = (lax.axis_index(a) for a in ("dp", "tx", "ty"))
    return dp // 2, dp % 2, tx, ty // 2, ty % 2


def peer(dy=0, dh=0, dz=0, dl=0, dc=0):
    y, h, z, l, c = place()
    return (
        lax.rem(y + dy, 4) * 2 + lax.rem(h + dh, 2),
        lax.rem(z + dz, 4),
        lax.rem(l + dl, 2) * 2 + lax.rem(c + dc, 2),
    )


def remote(src, dst, send, recv, to):
    return pltpu.make_async_remote_copy(
        src_ref=src, dst_ref=dst, send_sem=send, recv_sem=recv, device_id=to, device_id_type=MESH
    )


def landed(ref, sem):
    pltpu.make_async_copy(ref, ref, sem).wait()


def cols(i, n):
    return pl.ds(pl.multiple_of(i * n, n), n)


def standardize(tok_ref):
    values = tok_ref[...].astype(F32)
    average = jnp.mean(values, axis=-1, keepdims=True)
    centered = values - average
    spread = jnp.mean(centered * centered, axis=-1, keepdims=True)
    inv = lax.rsqrt(spread + 1e-06)
    return centered * inv, inv


def own_image(ref):
    _, _, z, _, _ = place()
    m = ref[...].astype(F32)
    first = (z < 2).astype(F32)
    return jnp.where(first > 0.5, m[0:1], m[1:2])


def slot(c, z, l):
    return c * 8 + z * 2 + l


def rows(c, z, l):
    return pl.ds(slot(c, z, l) * 32, 32)


PIECES = ((0, 0), (0, 1), (3, 0), (1, 0), (3, 1), (1, 1), (2, 0), (2, 1))
NF = 8
ND = 8
EARLY = 6


def block_kernel(
    tok_hbm, shift_hbm, scale_hbm, w_hbm, bias_hbm, act_hbm,
    token_grad, weight_grad, bias_grad, shift_grad, scale_grad,
    tok, shift, scale, bias, act, n, cb, w, g, gt, gb, sb, share, zs, zr, xs, xr, keep, xhat, inv,
    xw, bsum, brec, term, trec,
    in_sem, n_send, n_recv, c_send, c_recv, f_send, f_recv,
    y_send, y_recv, s_send, s_recv, z_send, z_recv, l_send, l_recv, x_send, x_recv,
    b_send, b_recv, t_send, t_recv,
):
    y, h, z, l, c = place()
    sib = peer(dc=1)
    pair = peer(dl=1)
    ring = {d: peer(dz=d) for d in (1, 2, 3)}
    group = {d: peer(dy=d) for d in (1, 2, 3)}
    cross = peer(dh=1)
    fc, dc = 1024 // NF, 8192 // ND

    loads = [
        pltpu.make_async_copy(src, dst, in_sem.at[k])
        for k, (src, dst) in enumerate(
            ((tok_hbm, tok), (shift_hbm, shift), (scale_hbm, scale), (bias_hbm, bias), (act_hbm, act), (w_hbm, w))
        )
    ]
    for cp in loads:
        cp.start()
    peers = [sib, pair, *ring.values(), *group.values(), cross]
    barrier = pltpu.get_barrier_semaphore()
    for p in peers:
        pl.semaphore_signal(barrier, inc=1, device_id=p, device_id_type=MESH)
    for cp in loads[:3]:
        cp.wait()
    xh, iv = standardize(tok)
    xhat[...] = xh
    inv[...] = jnp.broadcast_to(iv, inv.shape)
    n[rows(0, 0, 0), :] = (xh * (1.0 + own_image(scale)) + own_image(shift)).astype(BF16)
    pl.semaphore_wait(barrier, len(peers))

    pending = []

    def send(src, dst, to, half=None):
        s, d, sem = rows(*src), rows(*dst), slot(*dst)
        if half is not None:
            s = pl.ds(slot(*src) * 32 + half * 16, 16)
            d = pl.ds(slot(*dst) * 32 + half * 16, 16)
            sem = sem if half == 0 else 16 + dst[2]
        cp = remote(n.at[s], n.at[d], n_send.at[len(pending)], n_recv.at[sem], to)
        cp.start()
        pending.append(cp)

    def exchange(zz, ll):
        p = zz * 2 + ll
        for d in (2, 1, 3):
            block = lax.rem(y + d, 4)
            src = n.at[rows(0, zz, ll), cols(block, 2048)]
            cp = remote(
                src, cb.at[3 - d, rows(0, zz, ll)], c_send.at[d - 1, p], c_recv.at[3 - d, p], group[d]
            )
            cp.start()

    def arrived(*s):
        landed(n.at[rows(*s)], n_recv.at[slot(*s)])

    def block(zz):
        for ll in (0, 1):
            arrived(1, zz, ll)
        a, b = zz * 64, 256 + zz * 64
        at = []
        for cc in (0, 1):
            for ll in (0, 1):
                zr_ = lax.rem(z + zz, 4)
                at.append((zr_ * 4 + lax.rem(l + ll, 2) * 2 + lax.rem(c + cc, 2)) * 32)

        @pl.loop(0, 4)
        def _(j):
            t = cols(j, 256)
            x = jnp.concatenate([n[a : a + 64, :], n[b : b + 64, :]], axis=0)
            pre = jnp.dot(x, w[:, t], preferred_element_type=F32) + bias[:, t].astype(F32)
            up = jnp.concatenate([act[pl.ds(pl.multiple_of(r, 32), 32), t] for r in at], axis=0).astype(F32)
            sq = pre * pre
            th = jnp.tanh(GELU_A * pre * (1.0 + GELU_B * sq))
            slope = 0.5 * (1.0 + th) + 0.5 * GELU_A * pre * (1.0 - th * th) * (1.0 + 3.0 * GELU_B * sq)
            grad = (up * slope).astype(BF16)
            g[a : a + 64, t] = grad[0:64]
            g[b : b + 64, t] = grad[64:128]

    own = (0, 0, 0)
    send(own, (0, 0, 1), pair)
    send(own, (0, 3, 0), ring[1])
    send(own, (0, 1, 0), ring[3])
    send(own, (1, 0, 0), sib)
    exchange(0, 0)

    arrived(0, 0, 1)
    send((0, 0, 1), (0, 3, 1), ring[1])
    send((0, 0, 1), (0, 1, 1), ring[3])
    send((0, 0, 1), (1, 0, 1), sib)
    exchange(0, 1)
    for cp in loads[3:]:
        cp.wait()
    block(0)
    for ll in (0, 1):
        arrived(0, 3, ll)
        send((0, 3, ll), (0, 2, ll), ring[1], half=0)
        arrived(0, 1, ll)
        send((0, 1, ll), (0, 2, ll), ring[3], half=1)
        for zz in (3, 1):
            send((0, zz, ll), (1, zz, ll), sib)
            exchange(zz, ll)
    block(3)
    block(1)
    for ll in (0, 1):
        for half, sem in ((0, slot(0, 2, ll)), (1, 16 + ll)):
            landed(n.at[pl.ds(slot(0, 2, ll) * 32 + half * 16, 16)], n_recv.at[sem])
        send((0, 2, ll), (1, 2, ll), sib)
        exchange(2, ll)
    block(2)

    @pl.loop(0, 4)
    def _(j):
        gt[cols(j, 256), :] = g[:, cols(j, 256)].T

    def y_copy(d, q):
        return remote(
            gt.at[cols(q, fc)], gb.at[3 - d, cols(q, fc)], y_send.at[d - 1, q], y_recv.at[3 - d, q], group[d]
        )

    def y_start(q):
        for d in (2, 1, 3):
            y_copy(d, q).start()

    y_start(0)
    y_start(1)

    moved = []

    def pass_on(pieces):
        for zz, ll in pieces:
            p = zz * 2 + ll
            for s in range(3):
                src = cb.at[s, rows(0, zz, ll)]
                landed(src, c_recv.at[s, p])
                cp = remote(src, cb.at[s, rows(1, zz, ll)], f_send.at[s, p], f_recv.at[s, p], sib)
                cp.start()
                moved.append(cp)

    pass_on(PIECES[:6])

    def s_copy(j):
        k = lax.rem(j, 2)
        return remote(sb.at[k], share.at[pl.ds(2 * j, 2)], s_send.at[k], s_recv.at[j], sib)

    def z_copy(d, j):
        return remote(
            zs.at[pl.ds(d * 64, 64), cols(j, dc)],
            zr.at[3 - d, :, cols(j, dc)],
            z_send.at[d - 1, j],
            z_recv.at[3 - d, j],
            ring[d],
        )

    def core_sum(j):
        t = cols(j, dc)
        landed(share.at[pl.ds(2 * j, 2)], s_recv.at[j])
        theirs = share[pl.ds(2 * j, 2)].reshape(256, dc).astype(F32)
        zs[:, t] = (zs[:, t].astype(F32) + theirs).astype(BF16)
        for d in (2, 1, 3):
            z_copy(d, j).start()

    def normed_part(j):
        k = lax.rem(j, 2)

        @pl.when(j >= 2)
        def _():
            s_copy(j).wait_send()

        @pl.loop(0, dc // 512)
        def _(i):
            t = pl.ds(pl.multiple_of(j * dc + i * 512, 512), 512)
            p = lax.dot_general(g[...], w[t, :], (((1,), (1,)), ((), ())), preferred_element_type=F32)
            p = p.astype(BF16)
            zs[:, t] = p[0:256]
            sb[k, 0, :, cols(i, 512)] = p[256:384]
            sb[k, 1, :, cols(i, 512)] = p[384:512]

        s_copy(j).start()

        @pl.when(j >= 1)
        def _():
            core_sum(j - 1)

    pl.loop(0, EARLY)(normed_part)

    pass_on(PIECES[6:])
    pl.loop(2, NF)(y_start)

    pl.loop(EARLY, ND)(normed_part)
    core_sum(ND - 1)
    s_copy(0).wait_send()
    s_copy(1).wait_send()
    for cp in moved:
        cp.wait()

    def x_copy(q):
        return remote(share.at[q], xw.at[q], x_send.at[q], x_recv.at[q], cross)

    def l_copy(j):
        return remote(xs.at[:, cols(j, dc)], xr.at[:, cols(j, dc)], l_send.at[j], l_recv.at[j], pair)

    def weight_part(q):
        r = cols(q, fc)
        for s in range(3):
            landed(gb.at[s, r], y_recv.at[s, q])

        def tile(column):
            t = pl.ds(pl.multiple_of(column, 512), 512)
            own_t = pl.ds(pl.multiple_of(y * 2048 + column, 512), 512)
            acc = jnp.dot(gt[r, :], n[:, own_t], preferred_element_type=F32)
            for s in range(3):
                acc += jnp.dot(gb[s, r, :], cb[s, :, t], preferred_element_type=F32)
            return acc.astype(BF16)

        @pl.loop(0, 2)
        def _(i):
            share[q, :, cols(i, 512)] = tile((1 - h) * 1024 + i * 512)

        x_copy(q).start()

        @pl.loop(0, 2)
        def _(i):
            share[NF + q, :, cols(i, 512)] = tile(h * 1024 + i * 512)

        ones = jnp.ones((8, 512), BF16)
        nt = (((1,), (1,)), ((), ()))
        total = lax.dot_general(ones, gt[r, :], nt, preferred_element_type=F32)
        for s in range(3):
            total += lax.dot_general(ones, gb[s, r, :], nt, preferred_element_type=F32)
        bsum[:, r] = total

    def weight_sum(q):
        r = cols(q, fc)
        landed(xw.at[q], x_recv.at[q])
        weight_grad[:, r] = (share[NF + q].astype(F32) + xw[q].astype(F32)).T.astype(BF16)

    def z_sum(j):
        t = cols(j, dc)
        for s in range(3):
            landed(zr.at[s, :, t], z_recv.at[s, j])
        total = zs[0:64, t].astype(F32)
        for s in range(3):
            total += zr[s, :, t].astype(F32)
        keep[:, t] = total[0:32]
        xs[:, t] = total[32:64].astype(BF16)
        l_copy(j).start()

    def row_sum(j):
        t = cols(j, dc)
        landed(xr.at[:, t], l_recv.at[j])
        mine = keep[:, t] + xr[:, t].astype(F32)
        keep[:, t] = mine
        term[0, 0:1, t] = jnp.sum(mine, axis=0, keepdims=True)
        term[0, 1:2, t] = jnp.sum(mine * xhat[:, t], axis=0, keepdims=True)

    @pl.loop(0, NF)
    def _(q):
        weight_part(q)
        z_sum(q)

        @pl.when(q >= 1)
        def _():
            row_sum(q - 1)

        @pl.when(q >= 4)
        def _():
            weight_sum(q - 4)

    b_copy = remote(bsum, brec, b_send.at[0], b_recv.at[0], cross)
    b_copy.start()
    row_sum(ND - 1)

    near = (peer()[0], z + 1 - 2 * lax.rem(z, 2), peer()[2])
    hops = [
        remote(term.at[k], trec.at[k], t_send.at[k], t_recv.at[k], to)
        for k, to in enumerate((sib, pair, near, ring[2]))
    ]
    hops[0].start()

    scaled = keep[...] * (1.0 + own_image(scale))
    mean_one = jnp.mean(scaled, axis=-1, keepdims=True)
    mean_two = jnp.mean(scaled * xhat[...], axis=-1, keepdims=True)
    token_grad[...] = (inv[:, 0:1] * (scaled - mean_one - xhat[...] * mean_two)).astype(BF16)

    for k in range(3):
        hops[k].wait_recv()
        term[k + 1] = term[k] + trec[k]
        hops[k + 1].start()
        weight_sum(NF - 4 + k)
    b_copy.wait()
    bias_grad[...] = bsum[...] + brec[...]
    hops[3].wait_recv()
    first = (z < 2).astype(F32) > 0.5
    mine, other = term[3], trec[3]
    shift_grad[0:1, :] = jnp.where(first, mine[0:1], other[0:1])
    shift_grad[1:2, :] = jnp.where(first, other[0:1], mine[0:1])
    scale_grad[0:1, :] = jnp.where(first, mine[1:2], other[1:2])
    scale_grad[1:2, :] = jnp.where(first, other[1:2], mine[1:2])
    weight_sum(NF - 1)

    for k in range(4):
        hops[k].wait_send()
    for cp in pending:
        cp.wait_send()
    for zz, ll in PIECES:
        for s in range(3):
            landed(n.at[rows(0, zz, ll), pl.ds(0, 2048)], c_send.at[s, zz * 2 + ll])

    @pl.loop(0, NF)
    def _(q):
        for d in (1, 2, 3):
            y_copy(d, q).wait_send()
            z_copy(d, q).wait_send()
        l_copy(q).wait_send()
        x_copy(q).wait_send()


def result_kernel(a, b, c, d, e, ao, bo, co, do, eo, av, bv, cv, dv, ev, sem):
    held = (av, bv, cv, dv, ev)
    takes = [pltpu.make_async_copy(src, v, sem.at[k]) for k, (src, v) in enumerate(zip((a, b, c, d, e), held))]
    gives = [
        pltpu.make_async_copy(v, dst, sem.at[5 + k])
        for k, (v, dst) in enumerate(zip((av, bv, cv.at[0:1], dv, ev), (ao, bo, co, do, eo)))
    ]
    for cp in takes:
        cp.start()
    for cp, give in zip(takes, gives):
        cp.wait()
        give.start()
    for give in gives:
        give.wait()


def local(tokens, mod_shift, mod_scale, up_weight, up_bias, act_grad):
    vmem = pl.BlockSpec(memory_space=pltpu.VMEM)
    hbm = pl.BlockSpec(memory_space=pltpu.HBM)
    dma = pltpu.SemaphoreType.DMA
    results = (
        jax.ShapeDtypeStruct((32, 8192), BF16),
        jax.ShapeDtypeStruct((1024, 1024), BF16),
        jax.ShapeDtypeStruct((8, 1024), F32),
        jax.ShapeDtypeStruct((2, 8192), F32),
        jax.ShapeDtypeStruct((2, 8192), F32),
    )
    parts = pl.pallas_call(
        block_kernel,
        out_shape=results,
        in_specs=[hbm] * 6,
        out_specs=(vmem,) * 5,
        scratch_shapes=[
            pltpu.VMEM((32, 8192), BF16),
            pltpu.VMEM((2, 8192), BF16),
            pltpu.VMEM((2, 8192), BF16),
            pltpu.VMEM((1, 1024), BF16),
            pltpu.VMEM((512, 1024), BF16),
            pltpu.VMEM((512, 8192), BF16),
            pltpu.VMEM((3, 512, 2048), BF16),
            pltpu.VMEM((8192, 1024), BF16),
            pltpu.VMEM((512, 1024), BF16),
            pltpu.VMEM((1024, 512), BF16),
            pltpu.VMEM((3, 1024, 512), BF16),
            pltpu.VMEM((2, 2, 128, 1024), BF16),
            pltpu.VMEM((16, 128, 1024), BF16),
            pltpu.VMEM((256, 8192), BF16),
            pltpu.VMEM((3, 64, 8192), BF16),
            pltpu.VMEM((32, 8192), BF16),
            pltpu.VMEM((32, 8192), BF16),
            pltpu.VMEM((32, 8192), F32),
            pltpu.VMEM((32, 8192), F32),
            pltpu.VMEM((32, 128), F32),
            pltpu.VMEM((NF, 128, 1024), BF16),
            pltpu.VMEM((8, 1024), F32),
            pltpu.VMEM((8, 1024), F32),
            pltpu.VMEM((4, 2, 8192), F32),
            pltpu.VMEM((4, 2, 8192), F32),
            dma((6,)),
            dma((17,)),
            dma((18,)),
            dma((3, 8)),
            dma((3, 8)),
            dma((3, 8)),
            dma((3, 8)),
            dma((3, NF)),
            dma((3, NF)),
            dma((2,)),
            dma((ND,)),
            dma((3, ND)),
            dma((3, ND)),
            dma((ND,)),
            dma((ND,)),
            dma((NF,)),
            dma((NF,)),
            dma((1,)),
            dma((1,)),
            dma((4,)),
            dma((4,)),
        ],
        compiler_params=pltpu.CompilerParams(
            collective_id=0, has_side_effects=True, vmem_limit_bytes=61 * MIB
        ),
        name="block",
    )(tokens, mod_shift, mod_scale, up_weight, up_bias[None, :], act_grad)
    final = list(results)
    final[2] = jax.ShapeDtypeStruct((1, 1024), F32)
    token_grad, weight_grad, bias_grad, shift_grad, scale_grad = pl.pallas_call(
        result_kernel,
        out_shape=tuple(final),
        in_specs=[hbm] * 5,
        out_specs=(hbm,) * 5,
        scratch_shapes=[pltpu.VMEM(r.shape, r.dtype) for r in results] + [dma((10,))],
        compiler_params=pltpu.CompilerParams(vmem_limit_bytes=61 * MIB),
        name="results",
    )(*parts)
    return token_grad, weight_grad, bias_grad.reshape(1024), shift_grad, scale_grad


def solution(mesh):
    return jax.shard_map(
        local,
        mesh=mesh,
        in_specs=(
            P(("dp", "tx", "ty"), None),
            P("dp", None),
            P("dp", None),
            P(None, ("tx", "ty")),
            P(("tx", "ty")),
            P("dp", ("tx", "ty")),
        ),
        out_specs=(
            P(("dp", "tx", "ty"), None),
            P("dp", ("tx", "ty")),
            P(("tx", "ty")),
            P("dp", None),
            P("dp", None),
        ),
        check_vma=False,
    )
```

time: 193 us -> 147 us (0.76); the launches traced: 191 us -> 147 us
  Pallas kernels: 174 us -> 145 us
  local copies, waits for them, and re-layouts: 15.7 us -> 1.28 us
    pallas_call x2, Pallas kernels: 174 us -> 145 us  [the longest x1 142 us: local(): pl.pallas_call(block_kernel, out_shape=results, in_specs=[hbm] * 6, out_s...]
    unnamed x16 -> x0, local copies, waits for them, and re-layouts: 13.6 us -> none
where the time goes in v2:
time: 147 us
  Pallas kernels  145 us (99%)
    pallas_call x1, Pallas kernels, local(): pl.pallas_call(block_kernel, out_shape=results, in_specs=[hbm] * 6, out_s...  142 us
    pallas_call x1, Pallas kernels, local(): pl.pallas_call(result_kernel, out_shape=tuple(final), in_specs=[hbm] * 5,...  3.2 us

profile of v2, /device:TPU:0, one launch (start us, length us, event | category | flops | bytes accessed | tf_op | source)
XLA Modules:
  0.0 147.0 jit_solution(11256432071694010947)
XLA Ops:
  0.6 1.3 broadcast_in_dim.3.bias_hbm
  1.9 141.9 %block.1 = (bf16[32,8192]{1,0:T(8,128)(2,1)}, bf16[1024,1024]{1,0:T(8,128)(2,1)}, f32[8,1024]{1,0:T(8,128)}, f32[2,8192]{1,0:T(2,128)}, f32[2,8192]{1,0:T(2,128)}) custom-call(bf16[32,8192]{1,0:T(8,128)(2,1)} %tok_hbm.1, bf16[2,8192]{1,0:T(2,128)(2,1)} %shift_hbm.1, bf16[2,8192]{1,0:T(2,128)(2,1)} %scale_hbm.1, bf16[8192,1024]{1,0:T(8,128)(2,1)} %w_hbm.1, ...), custom_call_target="tpu_custom_call" | custom-call | tf_op jit(solution)/shard_map/block/pallas_call | solution.py:425
  143.8 3.2 %results.1 = (bf16[32,8192]{1,0:T(8,128)(2,1)}, bf16[1024,1024]{1,0:T(8,128)(2,1)}, f32[1,1024]{1,0:T(1,128)}, f32[2,8192]{1,0:T(2,128)}, f32[2,8192]{1,0:T(2,128)}) custom-call(bf16[32,8192]{1,0:T(8,128)(2,1)} %get-tuple-element.15.a, bf16[1024,1024]{1,0:T(8,128)(2,1)} %get-tuple-element.16.b, f32[8,1024]{1,0:T(8,128)} %get-tuple-element.17.c, ...), custom_call_target="tpu_custom_call" | custom-call | tf_op jit(solution)/shard_map/results/pallas_call | solution.py:485

commit v3 on v2

v3 whole, which is shorter than its diff:
```python
import jax
import jax.numpy as jnp
from jax import lax
from jax.experimental import pallas as pl
from jax.experimental.pallas import tpu as pltpu
from jax.sharding import PartitionSpec as P

MESH = pl.DeviceIdType.MESH
MIB = 1 << 20
F32 = jnp.float32
BF16 = jnp.bfloat16
GELU_A = 0.7978845608028654
GELU_B = 0.044715


def place():
    dp, tx, ty = (lax.axis_index(a) for a in ("dp", "tx", "ty"))
    return dp // 2, dp % 2, tx, ty // 2, ty % 2


def peer(dy=0, dh=0, dz=0, dl=0, dc=0):
    y, h, z, l, c = place()
    return (
        lax.rem(y + dy, 4) * 2 + lax.rem(h + dh, 2),
        lax.rem(z + dz, 4),
        lax.rem(l + dl, 2) * 2 + lax.rem(c + dc, 2),
    )


def remote(src, dst, send, recv, to):
    return pltpu.make_async_remote_copy(
        src_ref=src, dst_ref=dst, send_sem=send, recv_sem=recv, device_id=to, device_id_type=MESH
    )


def landed(ref, sem):
    pltpu.make_async_copy(ref, ref, sem).wait()


def cols(i, n):
    return pl.ds(pl.multiple_of(i * n, n), n)


def wide(x):
    return jnp.broadcast_to(x, (32, 128))


def slot(c, z, l):
    return c * 8 + z * 2 + l


def rows(c, z, l):
    return pl.ds(slot(c, z, l) * 32, 32)


SOON = ((0, 0), (0, 1), (3, 0), (1, 0))
LATE = ((3, 1), (1, 1), (2, 0), (2, 1))
NF = 8
ND = 8
AHEAD = 3


def block_kernel(
    tok_hbm, shift_hbm, scale_hbm, w_hbm, bias_hbm, act_hbm,
    token_hbm, weight_hbm, sums_hbm, shift_out, scale_out,
    tok, shift, scale, bias, n, cb, w, g, gt, sb, share, pw, zs, zr, xs, xr, keep, stats,
    xw, bsum, brec, term, trec, token_grad, weight_grad, shift_grad, scale_grad,
    in_sem, out_sem, wo_sem, own_sem, n_send, n_recv, c_send, c_recv, f_send, f_recv,
    y_send, y_recv, s_send, s_recv, z_send, z_recv, l_send, l_recv, x_send, x_recv,
    b_send, b_recv, t_send, t_recv,
):
    y, h, z, l, c = place()
    sib = peer(dc=1)
    pair = peer(dl=1)
    ring = {d: peer(dz=d) for d in (1, 2, 3)}
    group = {d: peer(dy=d) for d in (1, 2, 3)}
    cross = peer(dh=1)
    fc, dc = 1024 // NF, 8192 // ND

    loads = [
        pltpu.make_async_copy(src, dst, in_sem.at[k])
        for k, (src, dst) in enumerate(
            ((tok_hbm, tok), (shift_hbm, shift), (scale_hbm, scale), (bias_hbm, bias), (w_hbm, w))
        )
    ]
    for cc in (0, 1):
        for zz in range(4):
            for ll in (0, 1):
                r = (lax.rem(z + zz, 4) * 4 + lax.rem(l + ll, 2) * 2 + lax.rem(c + cc, 2)) * 32
                src = act_hbm.at[pl.ds(pl.multiple_of(r, 32), 32)]
                loads.append(pltpu.make_async_copy(src, g.at[rows(cc, zz, ll)], in_sem.at[len(loads)]))
    for cp in loads:
        cp.start()
    peers = [sib, pair, *ring.values(), *group.values(), cross]
    barrier = pltpu.get_barrier_semaphore()
    for p in peers:
        pl.semaphore_signal(barrier, inc=1, device_id=p, device_id_type=MESH)
    for cp in loads[:3]:
        cp.wait()

    def of_image(ref, t):
        m = ref[:, t].astype(F32)
        return jnp.where((z < 2).astype(F32) > 0.5, m[0:1], m[1:2])

    def row_total(f):
        def body(j, acc):
            return acc + jnp.sum(f(tok[:, cols(j, dc)].astype(F32)), axis=-1, keepdims=True)

        return lax.fori_loop(0, ND, body, jnp.zeros((32, 1), F32)) * (1.0 / 8192)

    average = row_total(lambda v: v)
    inverse = lax.rsqrt(row_total(lambda v: (v - average) * (v - average)) + 1e-06)
    stats[0] = wide(average)
    stats[1] = wide(inverse)
    stats[2] = jnp.zeros((32, 128), F32)
    stats[3] = jnp.zeros((32, 128), F32)

    def xhat(t):
        return (tok[:, t].astype(F32) - stats[0, :, 0:1]) * stats[1, :, 0:1]

    @pl.loop(0, ND)
    def _(j):
        t = cols(j, dc)
        n[rows(0, 0, 0), t] = (xhat(t) * (1.0 + of_image(scale, t)) + of_image(shift, t)).astype(BF16)

    pl.semaphore_wait(barrier, len(peers))

    pending = []

    def send(src, dst, to, half=None):
        s, d, sem = rows(*src), rows(*dst), slot(*dst)
        if half is not None:
            s = pl.ds(slot(*src) * 32 + half * 16, 16)
            d = pl.ds(slot(*dst) * 32 + half * 16, 16)
            sem = sem if half == 0 else 16 + dst[2]
        cp = remote(n.at[s], n.at[d], n_send.at[len(pending)], n_recv.at[sem], to)
        cp.start()
        pending.append(cp)

    def span(piece, part):
        k = piece[0] * 2 + piece[1]
        if part == "whole":
            return 0, 2048, k
        if part == "first":
            return (1 - h) * 1024, 1024, k
        return h * 1024, 1024, 8 + LATE.index(piece)

    def place_of(s, cc, piece, part):
        start, width, _ = span(piece, part)
        r = pl.ds(s * 512 + slot(cc, *piece) * 32, 32)
        return cb.at[r, pl.ds(pl.multiple_of(start, 1024), width)]

    def columns_copy(d, piece, part):
        start, width, k = span(piece, part)
        start = lax.rem(y + d, 4) * 2048 + start
        src = n.at[rows(0, *piece), pl.ds(pl.multiple_of(start, 1024), width)]
        dst = place_of(4 - d, 0, piece, part)
        return remote(src, dst, c_send.at[d - 1, k], c_recv.at[3 - d, k], group[d])

    sent = []

    def exchange(piece, part):
        for d in (2, 1, 3):
            cp = columns_copy(d, piece, part)
            cp.start()
            sent.append(cp)

    moved = []

    def pass_on(pieces, part):
        now = []
        for piece in pieces:
            k = span(piece, part)[2]
            for s in (1, 2, 3):
                src = place_of(s, 0, piece, part)
                landed(src, c_recv.at[s - 1, k])
                cp = remote(
                    src, place_of(s, 1, piece, part), f_send.at[s - 1, k], f_recv.at[s - 1, k], sib
                )
                cp.start()
                now.append(cp)
        moved.extend(now)
        return now

    def y_copy(d, q):
        return remote(
            gt.at[cols(q, fc), pl.ds(0, 512)],
            gt.at[cols(q, fc), pl.ds((4 - d) * 512, 512)],
            y_send.at[d - 1, q],
            y_recv.at[3 - d, q],
            group[d],
        )

    def y_start(q):
        for d in (2, 1, 3):
            y_copy(d, q).start()

    def arrived(*s):
        landed(n.at[rows(*s)], n_recv.at[slot(*s)])

    def block(zz, last=False):
        for ll in (0, 1):
            arrived(1, zz, ll)
        a, b = zz * 64, 256 + zz * 64

        @pl.loop(0, 4)
        def _(j):
            t = cols(j, 256)
            x = jnp.concatenate([n[a : a + 64, :], n[b : b + 64, :]], axis=0)
            pre = jnp.dot(x, w[:, t], preferred_element_type=F32) + bias[:, t].astype(F32)
            up = jnp.concatenate([g[a : a + 64, t], g[b : b + 64, t]], axis=0).astype(F32)
            sq = pre * pre
            th = jnp.tanh(GELU_A * pre * (1.0 + GELU_B * sq))
            slope = 0.5 * (1.0 + th) + 0.5 * GELU_A * pre * (1.0 - th * th) * (1.0 + 3.0 * GELU_B * sq)
            grad = (up * slope).astype(BF16)
            g[a : a + 64, t] = grad[0:64]
            g[b : b + 64, t] = grad[64:128]
            if last:
                gt[t, 0:512] = g[:, t].T

                @pl.when(j == 0)
                def _():
                    y_start(0)
                    y_start(1)

    own = (0, 0, 0)
    send(own, (0, 0, 1), pair)
    send(own, (0, 3, 0), ring[1])
    send(own, (0, 1, 0), ring[3])
    send(own, (1, 0, 0), sib)
    exchange((0, 0), "whole")

    arrived(0, 0, 1)
    send((0, 0, 1), (0, 3, 1), ring[1])
    send((0, 0, 1), (0, 1, 1), ring[3])
    send((0, 0, 1), (1, 0, 1), sib)
    exchange((0, 1), "whole")
    for cp in loads[3:]:
        cp.wait()
    block(0)
    for ll in (0, 1):
        arrived(0, 3, ll)
        send((0, 3, ll), (0, 2, ll), ring[1], half=0)
        arrived(0, 1, ll)
        send((0, 1, ll), (0, 2, ll), ring[3], half=1)
        for zz in (3, 1):
            send((0, zz, ll), (1, zz, ll), sib)
            exchange((zz, ll), "first" if ll else "whole")
    block(3)
    block(1)
    pass_on(SOON, "whole")
    for ll in (0, 1):
        for half, sem in ((0, slot(0, 2, ll)), (1, 16 + ll)):
            landed(n.at[pl.ds(slot(0, 2, ll) * 32 + half * 16, 16)], n_recv.at[sem])
        send((0, 2, ll), (1, 2, ll), sib)
        exchange((2, ll), "first")
    block(2, last=True)
    own_columns = pltpu.make_async_copy(n.at[:, cols(y, 2048)], cb.at[pl.ds(0, 512)], own_sem)
    own_columns.start()

    def s_copy(j):
        k = lax.rem(j, 2)
        return remote(sb.at[k], share.at[pl.ds(2 * j, 2)], s_send.at[k], s_recv.at[j], sib)

    def z_copy(d, j):
        return remote(
            zs.at[pl.ds(d * 64, 64), cols(j, dc)],
            zr.at[3 - d, :, cols(j, dc)],
            z_send.at[d - 1, j],
            z_recv.at[3 - d, j],
            ring[d],
        )

    def core_sum(j):
        t = cols(j, dc)
        landed(share.at[pl.ds(2 * j, 2)], s_recv.at[j])
        theirs = share[pl.ds(2 * j, 2)].reshape(256, dc).astype(F32)
        zs[:, t] = (zs[:, t].astype(F32) + theirs).astype(BF16)
        for d in (2, 1, 3):
            z_copy(d, j).start()

    def normed_part(j):
        k = lax.rem(j, 2)

        @pl.when(j >= 2)
        def _():
            s_copy(j).wait_send()

        @pl.loop(0, dc // 512)
        def _(i):
            t = pl.ds(pl.multiple_of(j * dc + i * 512, 512), 512)
            p = lax.dot_general(g[...], w[t, :], (((1,), (1,)), ((), ())), preferred_element_type=F32)
            p = p.astype(BF16)
            zs[:, t] = p[0:256]
            sb[k, 0, :, cols(i, 512)] = p[256:384]
            sb[k, 1, :, cols(i, 512)] = p[384:512]

        s_copy(j).start()

        @pl.when(j >= 1)
        def _():
            core_sum(j - 1)

    def x_copy(q):
        return remote(pw.at[q], xw.at[q], x_send.at[q], x_recv.at[q], cross)

    def l_copy(j):
        return remote(xs.at[:, cols(j, dc)], xr.at[:, cols(j, dc)], l_send.at[j], l_recv.at[j], pair)

    def weight_tile(q, column):
        t = pl.ds(pl.multiple_of(column, 512), 512)
        return jnp.dot(gt[cols(q, fc), :], cb[:, t], preferred_element_type=F32).astype(BF16)

    def weight_first(q):
        for s in (1, 2, 3):
            landed(gt.at[cols(q, fc), pl.ds(s * 512, 512)], y_recv.at[s - 1, q])

        @pl.loop(0, 2)
        def _(i):
            pw[q, :, cols(i, 512)] = weight_tile(q, (1 - h) * 1024 + i * 512)

        x_copy(q).start()

    def weight_second(q):
        @pl.loop(0, 2)
        def _(i):
            share[q, :, cols(i, 512)] = weight_tile(q, h * 1024 + i * 512)

        nt = (((1,), (1,)), ((), ()))
        bsum[:, cols(q, fc)] = lax.dot_general(
            jnp.ones((8, 2048), BF16), gt[cols(q, fc), :], nt, preferred_element_type=F32
        )

    def out_copy(q):
        k = lax.rem(q, 2)
        return pltpu.make_async_copy(weight_grad.at[k], weight_hbm.at[:, cols(q, fc)], wo_sem.at[k])

    def weight_sum(q):
        landed(xw.at[q], x_recv.at[q])

        @pl.when(q >= 2)
        def _():
            out_copy(q - 2).wait()

        weight_grad[lax.rem(q, 2)] = (share[q].astype(F32) + xw[q].astype(F32)).T.astype(BF16)
        out_copy(q).start()

    def z_sum(j):
        t = cols(j, dc)
        for s in range(3):
            landed(zr.at[s, :, t], z_recv.at[s, j])
        total = zs[0:64, t].astype(F32)
        for s in range(3):
            total += zr[s, :, t].astype(F32)
        keep[:, t] = total[0:32]
        xs[:, t] = total[32:64].astype(BF16)
        l_copy(j).start()

    def row_sum(j):
        t = cols(j, dc)
        landed(xr.at[:, t], l_recv.at[j])
        total = keep[:, t] + xr[:, t].astype(F32)
        keep[:, t] = total
        term[0, 0:1, t] = jnp.sum(total, axis=0, keepdims=True)
        hat = xhat(t)
        term[0, 1:2, t] = jnp.sum(total * hat, axis=0, keepdims=True)
        scaled = total * (1.0 + of_image(scale, t))
        stats[2] += wide(jnp.sum(scaled, axis=-1, keepdims=True))
        stats[3] += wide(jnp.sum(scaled * hat, axis=-1, keepdims=True))

    normed_part(0)
    pass_on(LATE, "first")
    pl.loop(1, AHEAD)(normed_part)
    own_columns.wait()
    for cp in moved:
        cp.wait()

    def step(q):
        weight_first(q)

        @pl.when(q + 2 < NF)
        def _():
            y_start(q + 2)

        @pl.when(q + AHEAD < ND)
        def _():
            normed_part(q + AHEAD)

        @pl.when(q + AHEAD == ND)
        def _():
            core_sum(ND - 1)

    step(0)
    for piece in LATE:
        exchange(piece, "second")
    step(1)
    for cp in pass_on(LATE, "second"):
        cp.wait()
    z_sum(0)

    @pl.loop(2, NF)
    def _(q):
        step(q)
        weight_second(q - 2)
        z_sum(q - 1)
        row_sum(q - 2)

        @pl.when(q >= 4)
        def _():
            weight_sum(q - 4)

    z_sum(ND - 1)
    weight_second(NF - 2)
    weight_second(NF - 1)
    b_copy = remote(bsum, brec, b_send.at[0], b_recv.at[0], cross)
    b_copy.start()
    row_sum(ND - 2)
    row_sum(ND - 1)

    near = (peer()[0], z + 1 - 2 * lax.rem(z, 2), peer()[2])
    hops = [
        remote(term.at[k], trec.at[k], t_send.at[k], t_recv.at[k], to)
        for k, to in enumerate((sib, pair, near, ring[2]))
    ]
    hops[0].start()

    @pl.loop(0, ND)
    def _(j):
        t = cols(j, dc)
        mean_one, mean_two = stats[2, :, 0:1] * (1.0 / 8192), stats[3, :, 0:1] * (1.0 / 8192)
        scaled = keep[:, t] * (1.0 + of_image(scale, t))
        token_grad[:, t] = (stats[1, :, 0:1] * (scaled - mean_one - xhat(t) * mean_two)).astype(BF16)

    outs = [
        pltpu.make_async_copy(src, dst, out_sem.at[k])
        for k, (src, dst) in enumerate(
            ((token_grad, token_hbm), (brec, sums_hbm), (shift_grad, shift_out), (scale_grad, scale_out))
        )
    ]
    outs[0].start()

    for k in range(3):
        hops[k].wait_recv()
        term[k + 1] = term[k] + trec[k]
        hops[k + 1].start()
        weight_sum(NF - 4 + k)
    b_copy.wait()
    brec[...] = bsum[...] + brec[...]
    outs[1].start()
    hops[3].wait_recv()
    first = (z < 2).astype(F32) > 0.5
    near_sum, far_sum = term[3], trec[3]
    shift_grad[0:1, :] = jnp.where(first, near_sum[0:1], far_sum[0:1])
    shift_grad[1:2, :] = jnp.where(first, far_sum[0:1], near_sum[0:1])
    scale_grad[0:1, :] = jnp.where(first, near_sum[1:2], far_sum[1:2])
    scale_grad[1:2, :] = jnp.where(first, far_sum[1:2], near_sum[1:2])
    outs[2].start()
    outs[3].start()
    weight_sum(NF - 1)

    for k in range(4):
        hops[k].wait_send()
    for cp in pending + sent:
        cp.wait_send()
    s_copy(0).wait_send()
    s_copy(1).wait_send()

    @pl.loop(0, NF)
    def _(q):
        for d in (1, 2, 3):
            y_copy(d, q).wait_send()
            z_copy(d, q).wait_send()
        l_copy(q).wait_send()
        x_copy(q).wait_send()

    out_copy(NF - 2).wait()
    out_copy(NF - 1).wait()
    for cp in outs:
        cp.wait()


def result_kernel(a, b, c, d, e, ao, bo, co, do, eo, av, bv, cv, dv, ev, sem):
    held = (av, bv, cv, dv, ev)
    takes = [pltpu.make_async_copy(src, v, sem.at[k]) for k, (src, v) in enumerate(zip((a, b, c, d, e), held))]
    gives = [
        pltpu.make_async_copy(v, dst, sem.at[5 + k])
        for k, (v, dst) in enumerate(zip((av, bv, cv.at[0:1], dv, ev), (ao, bo, co, do, eo)))
    ]
    for cp in takes:
        cp.start()
    for cp, give in zip(takes, gives):
        cp.wait()
        give.start()
    for give in gives:
        give.wait()


def local(tokens, mod_shift, mod_scale, up_weight, up_bias, act_grad):
    vmem = pl.BlockSpec(memory_space=pltpu.VMEM)
    hbm = pl.BlockSpec(memory_space=pltpu.HBM)
    dma = pltpu.SemaphoreType.DMA
    results = (
        jax.ShapeDtypeStruct((32, 8192), BF16),
        jax.ShapeDtypeStruct((1024, 1024), BF16),
        jax.ShapeDtypeStruct((8, 1024), F32),
        jax.ShapeDtypeStruct((2, 8192), F32),
        jax.ShapeDtypeStruct((2, 8192), F32),
    )
    parts = pl.pallas_call(
        block_kernel,
        out_shape=results,
        in_specs=[hbm] * 6,
        out_specs=(hbm,) * 5,
        scratch_shapes=[
            pltpu.VMEM((32, 8192), BF16),
            pltpu.VMEM((2, 8192), BF16),
            pltpu.VMEM((2, 8192), BF16),
            pltpu.VMEM((1, 1024), BF16),
            pltpu.VMEM((512, 8192), BF16),
            pltpu.VMEM((2048, 2048), BF16),
            pltpu.VMEM((8192, 1024), BF16),
            pltpu.VMEM((512, 1024), BF16),
            pltpu.VMEM((1024, 2048), BF16),
            pltpu.VMEM((2, 2, 128, 1024), BF16),
            pltpu.VMEM((16, 128, 1024), BF16),
            pltpu.VMEM((NF, 128, 1024), BF16),
            pltpu.VMEM((256, 8192), BF16),
            pltpu.VMEM((3, 64, 8192), BF16),
            pltpu.VMEM((32, 8192), BF16),
            pltpu.VMEM((32, 8192), BF16),
            pltpu.VMEM((32, 8192), F32),
            pltpu.VMEM((4, 32, 128), F32),
            pltpu.VMEM((NF, 128, 1024), BF16),
            pltpu.VMEM((8, 1024), F32),
            pltpu.VMEM((8, 1024), F32),
            pltpu.VMEM((4, 2, 8192), F32),
            pltpu.VMEM((4, 2, 8192), F32),
            pltpu.VMEM((32, 8192), BF16),
            pltpu.VMEM((2, 1024, 128), BF16),
            pltpu.VMEM((2, 8192), F32),
            pltpu.VMEM((2, 8192), F32),
            dma((21,)),
            dma((4,)),
            dma((2,)),
            dma(()),
            dma((17,)),
            dma((18,)),
            dma((3, 12)),
            dma((3, 12)),
            dma((3, 12)),
            dma((3, 12)),
            dma((3, NF)),
            dma((3, NF)),
            dma((2,)),
            dma((ND,)),
            dma((3, ND)),
            dma((3, ND)),
            dma((ND,)),
            dma((ND,)),
            dma((NF,)),
            dma((NF,)),
            dma((1,)),
            dma((1,)),
            dma((4,)),
            dma((4,)),
        ],
        compiler_params=pltpu.CompilerParams(
            collective_id=0, has_side_effects=True, vmem_limit_bytes=61 * MIB
        ),
        name="block",
    )(tokens, mod_shift, mod_scale, up_weight, up_bias[None, :], act_grad)
    final = list(results)
    final[2] = jax.ShapeDtypeStruct((1, 1024), F32)
    token_grad, weight_grad, bias_grad, shift_grad, scale_grad = pl.pallas_call(
        result_kernel,
        out_shape=tuple(final),
        in_specs=[hbm] * 5,
        out_specs=(hbm,) * 5,
        scratch_shapes=[pltpu.VMEM(r.shape, r.dtype) for r in results] + [dma((10,))],
        compiler_params=pltpu.CompilerParams(vmem_limit_bytes=61 * MIB),
        name="results",
    )(*parts)
    return token_grad, weight_grad, bias_grad.reshape(1024), shift_grad, scale_grad


def solution(mesh):
    return jax.shard_map(
        local,
        mesh=mesh,
        in_specs=(
            P(("dp", "tx", "ty"), None),
            P("dp", None),
            P("dp", None),
            P(None, ("tx", "ty")),
            P(("tx", "ty")),
            P("dp", ("tx", "ty")),
        ),
        out_specs=(
            P(("dp", "tx", "ty"), None),
            P("dp", ("tx", "ty")),
            P(("tx", "ty")),
            P("dp", None),
            P("dp", None),
        ),
        check_vma=False,
    )
```

time: 147 us -> 150 us (1.020)
  Pallas kernels: 145 us -> 148 us
    pallas_call x1, Pallas kernels: 142 us -> 145 us  [local(): pl.pallas_call(block_kernel, out_shape=results, in_specs=[hbm] * 6, out_s...]
where the time goes in v3:
time: 150 us
  Pallas kernels  148 us (99%)
    pallas_call x1, Pallas kernels, local(): pl.pallas_call(block_kernel, out_shape=results, in_specs=[hbm] * 6, out_s...  145 us
    pallas_call x1, Pallas kernels, local(): pl.pallas_call(result_kernel, out_shape=tuple(final), in_specs=[hbm] * 5,...  3.2 us

profile of v3, /device:TPU:0, one launch (start us, length us, event | category | flops | bytes accessed | tf_op | source)
XLA Modules:
  0.0 149.9 jit_solution(4612170081657027731)
XLA Ops:
  0.6 1.3 broadcast_in_dim.3.bias_hbm
  1.9 144.8 %block.1 = (bf16[32,8192]{1,0:T(8,128)(2,1)}, bf16[1024,1024]{1,0:T(8,128)(2,1)}, f32[8,1024]{1,0:T(8,128)}, f32[2,8192]{1,0:T(2,128)}, f32[2,8192]{1,0:T(2,128)}) custom-call(bf16[32,8192]{1,0:T(8,128)(2,1)} %tok_hbm.1, bf16[2,8192]{1,0:T(2,128)(2,1)} %shift_hbm.1, bf16[2,8192]{1,0:T(2,128)(2,1)} %scale_hbm.1, bf16[8192,1024]{1,0:T(8,128)(2,1)} %w_hbm.1, ...), custom_call_target="tpu_custom_call" | custom-call | tf_op jit(solution)/shard_map/block/pallas_call | solution.py:509
  146.7 3.2 %results.1 = (bf16[32,8192]{1,0:T(8,128)(2,1)}, bf16[1024,1024]{1,0:T(8,128)(2,1)}, f32[1,1024]{1,0:T(1,128)}, f32[2,8192]{1,0:T(2,128)}, f32[2,8192]{1,0:T(2,128)}) custom-call(bf16[32,8192]{1,0:T(8,128)(2,1)} %get-tuple-element.15.a, bf16[1024,1024]{1,0:T(8,128)(2,1)} %get-tuple-element.16.b, f32[8,1024]{1,0:T(8,128)} %get-tuple-element.17.c, ...), custom_call_target="tpu_custom_call" | custom-call | tf_op jit(solution)/shard_map/results/pallas_call | solution.py:574

commit v4 on v3

--- a/solution.py
+++ b/solution.py
@@ -127,15 +127,15 @@
 
     pending = []
 
-    def send(src, dst, to, half=None):
-        s, d, sem = rows(*src), rows(*dst), slot(*dst)
-        if half is not None:
-            s = pl.ds(slot(*src) * 32 + half * 16, 16)
-            d = pl.ds(slot(*dst) * 32 + half * 16, 16)
-            sem = sem if half == 0 else 16 + dst[2]
-        cp = remote(n.at[s], n.at[d], n_send.at[len(pending)], n_recv.at[sem], to)
-        cp.start()
-        pending.append(cp)
+    def half_rows(s, half):
+        return n.at[pl.ds(slot(*s) * 32 + half * 16, 16)]
+
+    def send(src, dst, to, halves=(0, 1)):
+        for half in halves:
+            sem = n_recv.at[slot(*dst) * 2 + half]
+            cp = remote(half_rows(src, half), half_rows(dst, half), n_send.at[len(pending)], sem, to)
+            cp.start()
+            pending.append(cp)
 
     def span(piece, part):
         k = piece[0] * 2 + piece[1]
@@ -183,38 +183,56 @@
         return now
 
     def y_copy(d, q):
+        r = cols(q, fc)
         return remote(
-            gt.at[cols(q, fc), pl.ds(0, 512)],
-            gt.at[cols(q, fc), pl.ds((4 - d) * 512, 512)],
-            y_send.at[d - 1, q],
+            gt.at[r, pl.ds(0, 512)],
+            gt.at[r, pl.ds((4 - d) * 512, 512)],
+            y_send.at[d // 2, q],
             y_recv.at[3 - d, q],
             group[d],
         )
 
+    def y_relay(d, q):
+        half = d // 2
+        r = pl.ds(pl.multiple_of(q * fc + half * (fc // 2), fc // 2), fc // 2)
+        return remote(
+            gt.at[r, pl.ds((4 - d) * 512, 512)],
+            gt.at[r, pl.ds(1024, 512)],
+            y_send.at[2 + half, q],
+            y_recv.at[1 if half == 0 else 3, q],
+            group[d],
+        )
+
     def y_start(q):
-        for d in (2, 1, 3):
+        for d in (1, 3):
             y_copy(d, q).start()
 
-    def arrived(*s):
-        landed(n.at[rows(*s)], n_recv.at[slot(*s)])
-
-    def block(zz, last=False):
-        for ll in (0, 1):
-            arrived(1, zz, ll)
-        a, b = zz * 64, 256 + zz * 64
+    def y_pass(q):
+        for d in (1, 3):
+            landed(gt.at[cols(q, fc), pl.ds((4 - d) * 512, 512)], y_recv.at[3 - d, q])
+            y_relay(d, q).start()
+
+    def arrived(s, halves=(0, 1)):
+        for half in halves:
+            landed(half_rows(s, half), n_recv.at[slot(*s) * 2 + half])
+
+    def block(pieces, last=False):
+        for piece in pieces:
+            arrived((1, *piece))
+        at = [rows(cc, *piece) for cc in (0, 1) for piece in pieces]
 
         @pl.loop(0, 4)
         def _(j):
             t = cols(j, 256)
-            x = jnp.concatenate([n[a : a + 64, :], n[b : b + 64, :]], axis=0)
+            x = jnp.concatenate([n[r, :] for r in at], axis=0)
             pre = jnp.dot(x, w[:, t], preferred_element_type=F32) + bias[:, t].astype(F32)
-            up = jnp.concatenate([g[a : a + 64, t], g[b : b + 64, t]], axis=0).astype(F32)
+            up = jnp.concatenate([g[r, t] for r in at], axis=0).astype(F32)
             sq = pre * pre
             th = jnp.tanh(GELU_A * pre * (1.0 + GELU_B * sq))
             slope = 0.5 * (1.0 + th) + 0.5 * GELU_A * pre * (1.0 - th * th) * (1.0 + 3.0 * GELU_B * sq)
             grad = (up * slope).astype(BF16)
-            g[a : a + 64, t] = grad[0:64]
-            g[b : b + 64, t] = grad[64:128]
+            for k, r in enumerate(at):
+                g[r, t] = grad[k * 32 : k * 32 + 32]
             if last:
                 gt[t, 0:512] = g[:, t].T
 
@@ -223,38 +241,51 @@
                     y_start(0)
                     y_start(1)
 
-    own = (0, 0, 0)
+    own, near_pair = (0, 0, 0), (0, 0, 1)
+    send(own, (0, 3, 0), ring[1], (0,))
+    send(own, (0, 1, 0), ring[3], (1,))
     send(own, (0, 0, 1), pair)
-    send(own, (0, 3, 0), ring[1])
-    send(own, (0, 1, 0), ring[3])
+    send(own, (0, 3, 0), ring[1], (1,))
+    send(own, (0, 1, 0), ring[3], (0,))
     send(own, (1, 0, 0), sib)
     exchange((0, 0), "whole")
 
-    arrived(0, 0, 1)
-    send((0, 0, 1), (0, 3, 1), ring[1])
-    send((0, 0, 1), (0, 1, 1), ring[3])
-    send((0, 0, 1), (1, 0, 1), sib)
-    exchange((0, 1), "whole")
+    def ring_piece(ll, part):
+        arrived((0, 3, ll), (0,))
+        send((0, 3, ll), (0, 2, ll), ring[1], (0,))
+        arrived((0, 1, ll), (1,))
+        send((0, 1, ll), (0, 2, ll), ring[3], (1,))
+        if ll == 0:
+            arrived(near_pair, (1,))
+            send(near_pair, (0, 1, 1), ring[3], (1,))
+            send(near_pair, (0, 3, 1), ring[1], (1,))
+            send(near_pair, (1, 0, 1), sib)
+            exchange((0, 1), "whole")
+        arrived((0, 3, ll), (1,))
+        arrived((0, 1, ll), (0,))
+        for zz in (3, 1):
+            send((0, zz, ll), (1, zz, ll), sib)
+            exchange((zz, ll), part)
+
+    def opposite_piece(ll):
+        arrived((0, 2, ll))
+        send((0, 2, ll), (1, 2, ll), sib)
+        exchange((2, ll), "first")
+
+    arrived(near_pair, (0,))
+    send(near_pair, (0, 3, 1), ring[1], (0,))
+    send(near_pair, (0, 1, 1), ring[3], (0,))
+    ring_piece(0, "whole")
     for cp in loads[3:]:
         cp.wait()
-    block(0)
-    for ll in (0, 1):
-        arrived(0, 3, ll)
-        send((0, 3, ll), (0, 2, ll), ring[1], half=0)
-        arrived(0, 1, ll)
-        send((0, 1, ll), (0, 2, ll), ring[3], half=1)
-        for zz in (3, 1):
-            send((0, zz, ll), (1, zz, ll), sib)
-            exchange((zz, ll), "first" if ll else "whole")
-    block(3)
-    block(1)
+    block(((0, 0), (0, 1)))
+    block(((3, 0), (1, 0)))
+    ring_piece(1, "first")
+    opposite_piece(0)
+    block(((3, 1), (1, 1)))
+    opposite_piece(1)
     pass_on(SOON, "whole")
-    for ll in (0, 1):
-        for half, sem in ((0, slot(0, 2, ll)), (1, 16 + ll)):
-            landed(n.at[pl.ds(slot(0, 2, ll) * 32 + half * 16, 16)], n_recv.at[sem])
-        send((0, 2, ll), (1, 2, ll), sib)
-        exchange((2, ll), "first")
-    block(2, last=True)
+    block(((2, 0), (2, 1)), last=True)
     own_columns = pltpu.make_async_copy(n.at[:, cols(y, 2048)], cb.at[pl.ds(0, 512)], own_sem)
     own_columns.start()
 
@@ -312,8 +343,9 @@
         return jnp.dot(gt[cols(q, fc), :], cb[:, t], preferred_element_type=F32).astype(BF16)
 
     def weight_first(q):
-        for s in (1, 2, 3):
-            landed(gt.at[cols(q, fc), pl.ds(s * 512, 512)], y_recv.at[s - 1, q])
+        for half in (0, 1):
+            r = pl.ds(pl.multiple_of(q * fc + half * (fc // 2), fc // 2), fc // 2)
+            landed(gt.at[r, pl.ds(1024, 512)], y_recv.at[1 + 2 * half, q])
 
         @pl.loop(0, 2)
         def _(i):
@@ -369,6 +401,7 @@
         stats[3] += wide(jnp.sum(scaled * hat, axis=-1, keepdims=True))
 
     normed_part(0)
+    y_pass(0)
     pass_on(LATE, "first")
     pl.loop(1, AHEAD)(normed_part)
     own_columns.wait()
@@ -378,43 +411,49 @@
     def step(q):
         weight_first(q)
 
+        @pl.when(q + 1 < NF)
+        def _():
+            y_pass(q + 1)
+
         @pl.when(q + 2 < NF)
         def _():
             y_start(q + 2)
 
-        @pl.when(q + AHEAD < ND)
-        def _():
-            normed_part(q + AHEAD)
-
-        @pl.when(q + AHEAD == ND)
+        j = AHEAD + 2 * q
+
+        @pl.when(j < ND)
+        def _():
+            normed_part(j)
+
+        @pl.when(j + 1 < ND)
+        def _():
+            normed_part(j + 1)
+
+        @pl.when(q == (ND - AHEAD + 1) // 2)
         def _():
             core_sum(ND - 1)
 
     step(0)
     for piece in LATE:
         exchange(piece, "second")
+    z_sum(0)
     step(1)
+    z_sum(1)
+    row_sum(0)
     for cp in pass_on(LATE, "second"):
         cp.wait()
-    z_sum(0)
 
     @pl.loop(2, NF)
     def _(q):
         step(q)
         weight_second(q - 2)
-        z_sum(q - 1)
-        row_sum(q - 2)
+        z_sum(q)
+        row_sum(q - 1)
 
         @pl.when(q >= 4)
         def _():
             weight_sum(q - 4)
 
-    z_sum(ND - 1)
-    weight_second(NF - 2)
-    weight_second(NF - 1)
-    b_copy = remote(bsum, brec, b_send.at[0], b_recv.at[0], cross)
-    b_copy.start()
-    row_sum(ND - 2)
     row_sum(ND - 1)
 
     near = (peer()[0], z + 1 - 2 * lax.rem(z, 2), peer()[2])
@@ -423,6 +462,13 @@
         for k, to in enumerate((sib, pair, near, ring[2]))
     ]
     hops[0].start()
+    weight_second(NF - 2)
+    weight_second(NF - 1)
+    b_copy = remote(bsum, brec, b_send.at[0], b_recv.at[0], cross)
+    b_copy.start()
+    hops[0].wait_recv()
+    term[1] = term[0] + trec[0]
+    hops[1].start()
 
     @pl.loop(0, ND)
     def _(j):
@@ -439,11 +485,11 @@
     ]
     outs[0].start()
 
-    for k in range(3):
+    for k in (1, 2):
         hops[k].wait_recv()
         term[k + 1] = term[k] + trec[k]
         hops[k + 1].start()
-        weight_sum(NF - 4 + k)
+        weight_sum(NF - 5 + k)
     b_copy.wait()
     brec[...] = bsum[...] + brec[...]
     outs[1].start()
@@ -456,6 +502,7 @@
     scale_grad[1:2, :] = jnp.where(first, far_sum[1:2], near_sum[1:2])
     outs[2].start()
     outs[3].start()
+    weight_sum(NF - 2)
     weight_sum(NF - 1)
 
     for k in range(4):
@@ -467,8 +514,10 @@
 
     @pl.loop(0, NF)
     def _(q):
+        for d in (1, 3):
+            y_copy(d, q).wait_send()
+            y_relay(d, q).wait_send()
         for d in (1, 2, 3):
-            y_copy(d, q).wait_send()
             z_copy(d, q).wait_send()
         l_copy(q).wait_send()
         x_copy(q).wait_send()
@@ -543,14 +592,14 @@
             dma((4,)),
             dma((2,)),
             dma(()),
-            dma((17,)),
-            dma((18,)),
+            dma((32,)),
+            dma((32,)),
             dma((3, 12)),
             dma((3, 12)),
             dma((3, 12)),
             dma((3, 12)),
-            dma((3, NF)),
-            dma((3, NF)),
+            dma((4, NF)),
+            dma((4, NF)),
             dma((2,)),
             dma((ND,)),
             dma((3, ND)),

time: 150 us -> 147 us (0.980)
  Pallas kernels: 148 us -> 145 us
    pallas_call x1, Pallas kernels: 145 us -> 141 us  [local(): pl.pallas_call(block_kernel, out_shape=results, in_specs=[hbm] * 6, out_s...]
where the time goes in v4:
time: 147 us
  Pallas kernels  145 us (99%)
    pallas_call x1, Pallas kernels, local(): pl.pallas_call(block_kernel, out_shape=results, in_specs=[hbm] * 6, out_s...  141 us
    pallas_call x1, Pallas kernels, local(): pl.pallas_call(result_kernel, out_shape=tuple(final), in_specs=[hbm] * 5,...  3.2 us

profile of v4, /device:TPU:0, one launch (start us, length us, event | category | flops | bytes accessed | tf_op | source)
XLA Modules:
  0.0 146.7 jit_solution(15009295302830192141)
XLA Ops:
  0.6 1.3 broadcast_in_dim.3.bias_hbm
  1.9 141.4 %block.1 = (bf16[32,8192]{1,0:T(8,128)(2,1)}, bf16[1024,1024]{1,0:T(8,128)(2,1)}, f32[8,1024]{1,0:T(8,128)}, f32[2,8192]{1,0:T(2,128)}, f32[2,8192]{1,0:T(2,128)}) custom-call(bf16[32,8192]{1,0:T(8,128)(2,1)} %tok_hbm.1, bf16[2,8192]{1,0:T(2,128)(2,1)} %shift_hbm.1, bf16[2,8192]{1,0:T(2,128)(2,1)} %scale_hbm.1, bf16[8192,1024]{1,0:T(8,128)(2,1)} %w_hbm.1, ...), custom_call_target="tpu_custom_call" | custom-call | tf_op jit(solution)/shard_map/block/pallas_call | solution.py:558
  143.4 3.2 %results.1 = (bf16[32,8192]{1,0:T(8,128)(2,1)}, bf16[1024,1024]{1,0:T(8,128)(2,1)}, f32[1,1024]{1,0:T(1,128)}, f32[2,8192]{1,0:T(2,128)}, f32[2,8192]{1,0:T(2,128)}) custom-call(bf16[32,8192]{1,0:T(8,128)(2,1)} %get-tuple-element.15.a, bf16[1024,1024]{1,0:T(8,128)(2,1)} %get-tuple-element.16.b, f32[8,1024]{1,0:T(8,128)} %get-tuple-element.17.c, ...), custom_call_target="tpu_custom_call" | custom-call | tf_op jit(solution)/shard_map/results/pallas_call | solution.py:623

commit v5 on v4

--- a/solution.py
+++ b/solution.py
@@ -41,6 +41,13 @@
     return pl.ds(pl.multiple_of(i * n, n), n)
 
 
+def lane_sums(x):
+    parts = [x[:, k : k + 128] for k in range(0, x.shape[1], 128)]
+    while len(parts) > 1:
+        parts = [a + b for a, b in zip(parts[::2], parts[1::2])]
+    return parts[0]
+
+
 def wide(x):
     return jnp.broadcast_to(x, (32, 128))
 
@@ -57,14 +64,14 @@
 LATE = ((3, 1), (1, 1), (2, 0), (2, 1))
 NF = 8
 ND = 8
-AHEAD = 3
+AHEAD = 4
 
 
 def block_kernel(
     tok_hbm, shift_hbm, scale_hbm, w_hbm, bias_hbm, act_hbm,
     token_hbm, weight_hbm, sums_hbm, shift_out, scale_out,
-    tok, shift, scale, bias, n, cb, w, g, gt, sb, share, pw, zs, zr, xs, xr, keep, stats,
-    xw, bsum, brec, term, trec, token_grad, weight_grad, shift_grad, scale_grad,
+    tok, shift, scale, bias, n, cb, w, g, gt, sb, share, zs, zr, xr, keep, stats,
+    xw, bsum, brec, term, trec, weight_grad, shift_grad, scale_grad,
     in_sem, out_sem, wo_sem, own_sem, n_send, n_recv, c_send, c_recv, f_send, f_recv,
     y_send, y_recv, s_send, s_recv, z_send, z_recv, l_send, l_recv, x_send, x_recv,
     b_send, b_recv, t_send, t_recv,
@@ -104,9 +111,10 @@
 
     def row_total(f):
         def body(j, acc):
-            return acc + jnp.sum(f(tok[:, cols(j, dc)].astype(F32)), axis=-1, keepdims=True)
-
-        return lax.fori_loop(0, ND, body, jnp.zeros((32, 1), F32)) * (1.0 / 8192)
+            return acc + lane_sums(f(tok[:, cols(j, dc)].astype(F32)))
+
+        acc = lax.fori_loop(0, ND, body, jnp.zeros((32, 128), F32))
+        return jnp.sum(acc, axis=-1, keepdims=True) * (1.0 / 8192)
 
     average = row_total(lambda v: v)
     inverse = lax.rsqrt(row_total(lambda v: (v - average) * (v - average)) + 1e-06)
@@ -163,7 +171,8 @@
         for d in (2, 1, 3):
             cp = columns_copy(d, piece, part)
             cp.start()
-            sent.append(cp)
+            if part != "second":
+                sent.append(cp)
 
     moved = []
 
@@ -221,9 +230,9 @@
             arrived((1, *piece))
         at = [rows(cc, *piece) for cc in (0, 1) for piece in pieces]
 
-        @pl.loop(0, 4)
+        @pl.loop(0, 2)
         def _(j):
-            t = cols(j, 256)
+            t = cols(j, 512)
             x = jnp.concatenate([n[r, :] for r in at], axis=0)
             pre = jnp.dot(x, w[:, t], preferred_element_type=F32) + bias[:, t].astype(F32)
             up = jnp.concatenate([g[r, t] for r in at], axis=0).astype(F32)
@@ -240,6 +249,7 @@
                 def _():
                     y_start(0)
                     y_start(1)
+                    y_start(2)
 
     own, near_pair = (0, 0, 0), (0, 0, 1)
     send(own, (0, 3, 0), ring[1], (0,))
@@ -332,14 +342,17 @@
         def _():
             core_sum(j - 1)
 
+    def part(q):
+        return (16 + q) % 19
+
     def x_copy(q):
-        return remote(pw.at[q], xw.at[q], x_send.at[q], x_recv.at[q], cross)
+        return remote(share.at[part(q)], xw.at[q], x_send.at[q], x_recv.at[q], cross)
 
     def l_copy(j):
-        return remote(xs.at[:, cols(j, dc)], xr.at[:, cols(j, dc)], l_send.at[j], l_recv.at[j], pair)
+        return remote(zs.at[pl.ds(32, 32), cols(j, dc)], xr.at[:, cols(j, dc)], l_send.at[j], l_recv.at[j], pair)
 
     def weight_tile(q, column):
-        t = pl.ds(pl.multiple_of(column, 512), 512)
+        t = pl.ds(pl.multiple_of(column, 1024), 1024)
         return jnp.dot(gt[cols(q, fc), :], cb[:, t], preferred_element_type=F32).astype(BF16)
 
     def weight_first(q):
@@ -347,21 +360,11 @@
             r = pl.ds(pl.multiple_of(q * fc + half * (fc // 2), fc // 2), fc // 2)
             landed(gt.at[r, pl.ds(1024, 512)], y_recv.at[1 + 2 * half, q])
 
-        @pl.loop(0, 2)
-        def _(i):
-            pw[q, :, cols(i, 512)] = weight_tile(q, (1 - h) * 1024 + i * 512)
-
+        share[part(q)] = weight_tile(q, (1 - h) * 1024)
         x_copy(q).start()
 
     def weight_second(q):
-        @pl.loop(0, 2)
-        def _(i):
-            share[q, :, cols(i, 512)] = weight_tile(q, h * 1024 + i * 512)
-
-        nt = (((1,), (1,)), ((), ()))
-        bsum[:, cols(q, fc)] = lax.dot_general(
-            jnp.ones((8, 2048), BF16), gt[cols(q, fc), :], nt, preferred_element_type=F32
-        )
+        share[NF + q] = weight_tile(q, h * 1024)
 
     def out_copy(q):
         k = lax.rem(q, 2)
@@ -374,7 +377,7 @@
         def _():
             out_copy(q - 2).wait()
 
-        weight_grad[lax.rem(q, 2)] = (share[q].astype(F32) + xw[q].astype(F32)).T.astype(BF16)
+        weight_grad[lax.rem(q, 2)] = (share[NF + q].astype(F32) + xw[q].astype(F32)).T.astype(BF16)
         out_copy(q).start()
 
     def z_sum(j):
@@ -385,7 +388,7 @@
         for s in range(3):
             total += zr[s, :, t].astype(F32)
         keep[:, t] = total[0:32]
-        xs[:, t] = total[32:64].astype(BF16)
+        zs[32:64, t] = total[32:64].astype(BF16)
         l_copy(j).start()
 
     def row_sum(j):
@@ -397,13 +400,14 @@
         hat = xhat(t)
         term[0, 1:2, t] = jnp.sum(total * hat, axis=0, keepdims=True)
         scaled = total * (1.0 + of_image(scale, t))
-        stats[2] += wide(jnp.sum(scaled, axis=-1, keepdims=True))
-        stats[3] += wide(jnp.sum(scaled * hat, axis=-1, keepdims=True))
-
-    normed_part(0)
+        stats[2] += lane_sums(scaled)
+        stats[3] += lane_sums(scaled * hat)
+
+    pl.loop(0, AHEAD - 1)(normed_part)
     y_pass(0)
     pass_on(LATE, "first")
-    pl.loop(1, AHEAD)(normed_part)
+    y_pass(1)
+    normed_part(AHEAD - 1)
     own_columns.wait()
     for cp in moved:
         cp.wait()
@@ -411,13 +415,13 @@
     def step(q):
         weight_first(q)
 
-        @pl.when(q + 1 < NF)
-        def _():
-            y_pass(q + 1)
-
         @pl.when(q + 2 < NF)
         def _():
-            y_start(q + 2)
+            y_pass(q + 2)
+
+        @pl.when(q + 3 < NF)
+        def _():
+            y_start(q + 3)
 
         j = AHEAD + 2 * q
 
@@ -433,27 +437,49 @@
         def _():
             core_sum(ND - 1)
 
-    step(0)
-    for piece in LATE:
-        exchange(piece, "second")
-    z_sum(0)
-    step(1)
-    z_sum(1)
-    row_sum(0)
-    for cp in pass_on(LATE, "second"):
-        cp.wait()
-
-    @pl.loop(2, NF)
+    def rows_step(q):
+        @pl.when(q >= 1)
+        def _():
+            z_sum(q - 1)
+
+        @pl.when(q >= 2)
+        def _():
+            row_sum(q - 2)
+
+    @pl.loop(0, 5)
     def _(q):
         step(q)
-        weight_second(q - 2)
-        z_sum(q)
-        row_sum(q - 1)
-
-        @pl.when(q >= 4)
-        def _():
-            weight_sum(q - 4)
-
+        for k, piece in enumerate(LATE):
+
+            @pl.when(q == 1 + k)
+            def _():
+                exchange(piece, "second")
+
+        rows_step(q)
+
+    second = pass_on(LATE, "second")
+
+    @pl.loop(5, NF)
+    def _(q):
+        step(q)
+
+        @pl.when(q == 5)
+        def _():
+            for cp in second:
+                cp.wait()
+
+        for k in range(3):
+            p = 3 * (q - 5) + k
+
+            @pl.when(p < NF)
+            def _():
+                weight_second(p)
+
+        rows_step(q)
+        weight_sum(q - 5)
+
+    z_sum(ND - 1)
+    row_sum(ND - 2)
     row_sum(ND - 1)
 
     near = (peer()[0], z + 1 - 2 * lax.rem(z, 2), peer()[2])
@@ -462,25 +488,28 @@
         for k, to in enumerate((sib, pair, near, ring[2]))
     ]
     hops[0].start()
-    weight_second(NF - 2)
-    weight_second(NF - 1)
+    nt = (((1,), (1,)), ((), ()))
+    bsum[...] = lax.dot_general(jnp.ones((8, 2048), BF16), gt[...], nt, preferred_element_type=F32)
     b_copy = remote(bsum, brec, b_send.at[0], b_recv.at[0], cross)
     b_copy.start()
     hops[0].wait_recv()
     term[1] = term[0] + trec[0]
     hops[1].start()
 
+    stats[2] = wide(jnp.sum(stats[2], axis=-1, keepdims=True) * (1.0 / 8192))
+    stats[3] = wide(jnp.sum(stats[3], axis=-1, keepdims=True) * (1.0 / 8192))
+
     @pl.loop(0, ND)
     def _(j):
         t = cols(j, dc)
-        mean_one, mean_two = stats[2, :, 0:1] * (1.0 / 8192), stats[3, :, 0:1] * (1.0 / 8192)
+        mean_one, mean_two = stats[2, :, 0:1], stats[3, :, 0:1]
         scaled = keep[:, t] * (1.0 + of_image(scale, t))
-        token_grad[:, t] = (stats[1, :, 0:1] * (scaled - mean_one - xhat(t) * mean_two)).astype(BF16)
+        xr[:, t] = (stats[1, :, 0:1] * (scaled - mean_one - xhat(t) * mean_two)).astype(BF16)
 
     outs = [
         pltpu.make_async_copy(src, dst, out_sem.at[k])
         for k, (src, dst) in enumerate(
-            ((token_grad, token_hbm), (brec, sums_hbm), (shift_grad, shift_out), (scale_grad, scale_out))
+            ((xr, token_hbm), (brec, sums_hbm), (shift_grad, shift_out), (scale_grad, scale_out))
         )
     ]
     outs[0].start()
@@ -489,7 +518,7 @@
         hops[k].wait_recv()
         term[k + 1] = term[k] + trec[k]
         hops[k + 1].start()
-        weight_sum(NF - 5 + k)
+        weight_sum(2 + k)
     b_copy.wait()
     brec[...] = bsum[...] + brec[...]
     outs[1].start()
@@ -502,12 +531,12 @@
     scale_grad[1:2, :] = jnp.where(first, far_sum[1:2], near_sum[1:2])
     outs[2].start()
     outs[3].start()
-    weight_sum(NF - 2)
-    weight_sum(NF - 1)
+    for q in (5, 6, 7):
+        weight_sum(q)
 
     for k in range(4):
         hops[k].wait_send()
-    for cp in pending + sent:
+    for cp in pending + sent + [columns_copy(d, piece, "second") for piece in LATE for d in (1, 2, 3)]:
         cp.wait_send()
     s_copy(0).wait_send()
     s_copy(1).wait_send()
@@ -571,11 +600,9 @@
             pltpu.VMEM((512, 1024), BF16),
             pltpu.VMEM((1024, 2048), BF16),
             pltpu.VMEM((2, 2, 128, 1024), BF16),
-            pltpu.VMEM((16, 128, 1024), BF16),
-            pltpu.VMEM((NF, 128, 1024), BF16),
+            pltpu.VMEM((19, 128, 1024), BF16),
             pltpu.VMEM((256, 8192), BF16),
             pltpu.VMEM((3, 64, 8192), BF16),
-            pltpu.VMEM((32, 8192), BF16),
             pltpu.VMEM((32, 8192), BF16),
             pltpu.VMEM((32, 8192), F32),
             pltpu.VMEM((4, 32, 128), F32),
@@ -584,7 +611,6 @@
             pltpu.VMEM((8, 1024), F32),
             pltpu.VMEM((4, 2, 8192), F32),
             pltpu.VMEM((4, 2, 8192), F32),
-            pltpu.VMEM((32, 8192), BF16),
             pltpu.VMEM((2, 1024, 128), BF16),
             pltpu.VMEM((2, 8192), F32),
             pltpu.VMEM((2, 8192), F32),

time: 147 us -> 143 us (0.973)
  Pallas kernels: 145 us -> 140 us
    pallas_call x1, Pallas kernels: 141 us -> 137 us  [local(): pl.pallas_call(block_kernel, out_shape=results, in_specs=[hbm] * 6, out_s...]
where the time goes in v5:
time: 143 us
  Pallas kernels  140 us (98%)
    pallas_call x1, Pallas kernels, local(): pl.pallas_call(block_kernel, out_shape=results, in_specs=[hbm] * 6, out_s...  137 us
    pallas_call x1, Pallas kernels, local(): pl.pallas_call(result_kernel, out_shape=tuple(final), in_specs=[hbm] * 5,...  3.2 us

profile of v5, /device:TPU:0, one launch (start us, length us, event | category | flops | bytes accessed | tf_op | source)
XLA Modules:
  0.0 142.6 jit_solution(14573558589663681604)
XLA Ops:
  0.6 1.3 broadcast_in_dim.3.bias_hbm
  1.9 137.3 %block.1 = (bf16[32,8192]{1,0:T(8,128)(2,1)}, bf16[1024,1024]{1,0:T(8,128)(2,1)}, f32[8,1024]{1,0:T(8,128)}, f32[2,8192]{1,0:T(2,128)}, f32[2,8192]{1,0:T(2,128)}) custom-call(bf16[32,8192]{1,0:T(8,128)(2,1)} %tok_hbm.1, bf16[2,8192]{1,0:T(2,128)(2,1)} %shift_hbm.1, bf16[2,8192]{1,0:T(2,128)(2,1)} %scale_hbm.1, bf16[8192,1024]{1,0:T(8,128)(2,1)} %w_hbm.1, ...), custom_call_target="tpu_custom_call" | custom-call | tf_op jit(solution)/shard_map/block/pallas_call | solution.py:587
  139.2 3.2 %results.1 = (bf16[32,8192]{1,0:T(8,128)(2,1)}, bf16[1024,1024]{1,0:T(8,128)(2,1)}, f32[1,1024]{1,0:T(1,128)}, f32[2,8192]{1,0:T(2,128)}, f32[2,8192]{1,0:T(2,128)}) custom-call(bf16[32,8192]{1,0:T(8,128)(2,1)} %get-tuple-element.15.a, bf16[1024,1024]{1,0:T(8,128)(2,1)} %get-tuple-element.16.b, f32[8,1024]{1,0:T(8,128)} %get-tuple-element.17.c, ...), custom_call_target="tpu_custom_call" | custom-call | tf_op jit(solution)/shard_map/results/pallas_call | solution.py:649

commit v6 on v5

--- a/solution.py
+++ b/solution.py
@@ -64,7 +64,7 @@
 LATE = ((3, 1), (1, 1), (2, 0), (2, 1))
 NF = 8
 ND = 8
-AHEAD = 4
+BLOCKS = (((0, 0), (0, 1)), ((3, 0), (1, 0)), ((3, 1), (1, 1)), ((2, 0), (2, 1)))
 
 
 def block_kernel(
@@ -73,7 +73,7 @@
     tok, shift, scale, bias, n, cb, w, g, gt, sb, share, zs, zr, xr, keep, stats,
     xw, bsum, brec, term, trec, weight_grad, shift_grad, scale_grad,
     in_sem, out_sem, wo_sem, own_sem, n_send, n_recv, c_send, c_recv, f_send, f_recv,
-    y_send, y_recv, s_send, s_recv, z_send, z_recv, l_send, l_recv, x_send, x_recv,
+    y_send, y_recv, s_send, s_recv, zw_send, zw_recv, z_send, z_recv, l_send, l_recv, x_send, x_recv,
     b_send, b_recv, t_send, t_recv,
 ):
     y, h, z, l, c = place()
@@ -251,6 +251,55 @@
                     y_start(1)
                     y_start(2)
 
+    def s_copy(b, j):
+        there = share.at[2 * j + b // 2, pl.ds((b % 2) * 64, 64)]
+        return remote(sb.at[j], there, s_send.at[j], s_recv.at[b, j], sib)
+
+    def z_whole(zz, ll):
+        k = (zz // 2) * 2 + ll
+        there = zr.at[3 - zz, pl.ds(ll * 32, 32)]
+        return remote(zs.at[rows(0, zz, ll)], there, zw_send.at[k], zw_recv.at[k], ring[zz])
+
+    def z_far(j):
+        t = cols(j, dc)
+        return remote(zs.at[pl.ds(128, 64), t], zr.at[1, :, t], z_send.at[j], z_recv.at[j], ring[2])
+
+    def core_sum(b, j):
+        t = cols(j, dc)
+        unit, first_row = 2 * j + b // 2, (b % 2) * 64
+        landed(share.at[unit, pl.ds(first_row, 64)], s_recv.at[b, j])
+        for k, piece in enumerate(BLOCKS[b]):
+            theirs = share[unit, first_row + k * 32 : first_row + k * 32 + 32].astype(F32)
+            zs[rows(0, *piece), t] = (zs[rows(0, *piece), t].astype(F32) + theirs).astype(BF16)
+        if b == 3:
+            z_far(j).start()
+
+    def normed(b):
+        at = [rows(cc, *piece) for cc in (0, 1) for piece in BLOCKS[b]]
+
+        @pl.loop(0, ND)
+        def _(j):
+            if b > 0:
+                s_copy(b - 1, j).wait_send()
+
+            @pl.loop(0, dc // 512)
+            def _(i):
+                t = pl.ds(pl.multiple_of(j * dc + i * 512, 512), 512)
+                x = jnp.concatenate([g[r, :] for r in at], axis=0)
+                p = lax.dot_general(x, w[t, :], (((1,), (1,)), ((), ())), preferred_element_type=F32)
+                p = p.astype(BF16)
+                for k, piece in enumerate(BLOCKS[b]):
+                    zs[rows(0, *piece), t] = p[k * 32 : k * 32 + 32]
+                sb[j, :, cols(i, 512)] = p[64:128]
+
+            s_copy(b, j).start()
+
+            @pl.when(j >= 1)
+            def _():
+                core_sum(b, j - 1)
+
+        core_sum(b, ND - 1)
+
     own, near_pair = (0, 0, 0), (0, 0, 1)
     send(own, (0, 3, 0), ring[1], (0,))
     send(own, (0, 1, 0), ring[3], (1,))
@@ -260,11 +309,13 @@
     send(own, (1, 0, 0), sib)
     exchange((0, 0), "whole")
 
-    def ring_piece(ll, part):
+    def ring_piece(ll):
         arrived((0, 3, ll), (0,))
         send((0, 3, ll), (0, 2, ll), ring[1], (0,))
         arrived((0, 1, ll), (1,))
         send((0, 1, ll), (0, 2, ll), ring[3], (1,))
+
+    def ring_rest(ll, part):
         if ll == 0:
             arrived(near_pair, (1,))
             send(near_pair, (0, 1, 1), ring[3], (1,))
@@ -285,62 +336,25 @@
     arrived(near_pair, (0,))
     send(near_pair, (0, 3, 1), ring[1], (0,))
     send(near_pair, (0, 1, 1), ring[3], (0,))
-    ring_piece(0, "whole")
+    ring_piece(0)
+    ring_rest(0, "whole")
     for cp in loads[3:]:
         cp.wait()
-    block(((0, 0), (0, 1)))
-    block(((3, 0), (1, 0)))
-    ring_piece(1, "first")
+    block(BLOCKS[0])
+    block(BLOCKS[1])
+    ring_piece(1)
+    normed(0)
+    normed(1)
+    ring_rest(1, "first")
     opposite_piece(0)
-    block(((3, 1), (1, 1)))
+    block(BLOCKS[2])
     opposite_piece(1)
+    z_whole(3, 0).start()
+    z_whole(1, 0).start()
     pass_on(SOON, "whole")
-    block(((2, 0), (2, 1)), last=True)
+    block(BLOCKS[3], last=True)
     own_columns = pltpu.make_async_copy(n.at[:, cols(y, 2048)], cb.at[pl.ds(0, 512)], own_sem)
     own_columns.start()
-
-    def s_copy(j):
-        k = lax.rem(j, 2)
-        return remote(sb.at[k], share.at[pl.ds(2 * j, 2)], s_send.at[k], s_recv.at[j], sib)
-
-    def z_copy(d, j):
-        return remote(
-            zs.at[pl.ds(d * 64, 64), cols(j, dc)],
-            zr.at[3 - d, :, cols(j, dc)],
-            z_send.at[d - 1, j],
-            z_recv.at[3 - d, j],
-            ring[d],
-        )
-
-    def core_sum(j):
-        t = cols(j, dc)
-        landed(share.at[pl.ds(2 * j, 2)], s_recv.at[j])
-        theirs = share[pl.ds(2 * j, 2)].reshape(256, dc).astype(F32)
-        zs[:, t] = (zs[:, t].astype(F32) + theirs).astype(BF16)
-        for d in (2, 1, 3):
-            z_copy(d, j).start()
-
-    def normed_part(j):
-        k = lax.rem(j, 2)
-
-        @pl.when(j >= 2)
-        def _():
-            s_copy(j).wait_send()
-
-        @pl.loop(0, dc // 512)
-        def _(i):
-            t = pl.ds(pl.multiple_of(j * dc + i * 512, 512), 512)
-            p = lax.dot_general(g[...], w[t, :], (((1,), (1,)), ((), ())), preferred_element_type=F32)
-            p = p.astype(BF16)
-            zs[:, t] = p[0:256]
-            sb[k, 0, :, cols(i, 512)] = p[256:384]
-            sb[k, 1, :, cols(i, 512)] = p[384:512]
-
-        s_copy(j).start()
-
-        @pl.when(j >= 1)
-        def _():
-            core_sum(j - 1)
 
     def part(q):
         return (16 + q) % 19
@@ -382,8 +396,7 @@
 
     def z_sum(j):
         t = cols(j, dc)
-        for s in range(3):
-            landed(zr.at[s, :, t], z_recv.at[s, j])
+        landed(zr.at[1, :, t], z_recv.at[j])
         total = zs[0:64, t].astype(F32)
         for s in range(3):
             total += zr[s, :, t].astype(F32)
@@ -403,11 +416,13 @@
         stats[2] += lane_sums(scaled)
         stats[3] += lane_sums(scaled * hat)
 
-    pl.loop(0, AHEAD - 1)(normed_part)
+    normed(2)
+    z_whole(3, 1).start()
+    z_whole(1, 1).start()
     y_pass(0)
     pass_on(LATE, "first")
+    normed(3)
     y_pass(1)
-    normed_part(AHEAD - 1)
     own_columns.wait()
     for cp in moved:
         cp.wait()
@@ -423,28 +438,22 @@
         def _():
             y_start(q + 3)
 
-        j = AHEAD + 2 * q
-
-        @pl.when(j < ND)
+    def rows_step(q):
+        @pl.when(q == 3)
         def _():
-            normed_part(j)
-
-        @pl.when(j + 1 < ND)
+            for zz in (1, 3):
+                for ll in (0, 1):
+                    landed(zr.at[3 - zz, pl.ds(ll * 32, 32)], zw_recv.at[(zz // 2) * 2 + ll])
+
+        @pl.when((q >= 3) & (q <= 6))
         def _():
-            normed_part(j + 1)
-
-        @pl.when(q == (ND - AHEAD + 1) // 2)
+            z_sum(2 * q - 6)
+            z_sum(2 * q - 5)
+
+        @pl.when(q >= 4)
         def _():
-            core_sum(ND - 1)
-
-    def rows_step(q):
-        @pl.when(q >= 1)
-        def _():
-            z_sum(q - 1)
-
-        @pl.when(q >= 2)
-        def _():
-            row_sum(q - 2)
+            row_sum(2 * q - 8)
+            row_sum(2 * q - 7)
 
     @pl.loop(0, 5)
     def _(q):
@@ -478,9 +487,6 @@
         rows_step(q)
         weight_sum(q - 5)
 
-    z_sum(ND - 1)
-    row_sum(ND - 2)
-    row_sum(ND - 1)
 
     near = (peer()[0], z + 1 - 2 * lax.rem(z, 2), peer()[2])
     hops = [
@@ -538,16 +544,17 @@
         hops[k].wait_send()
     for cp in pending + sent + [columns_copy(d, piece, "second") for piece in LATE for d in (1, 2, 3)]:
         cp.wait_send()
-    s_copy(0).wait_send()
-    s_copy(1).wait_send()
+    for zz in (1, 3):
+        for ll in (0, 1):
+            z_whole(zz, ll).wait_send()
 
     @pl.loop(0, NF)
     def _(q):
         for d in (1, 3):
             y_copy(d, q).wait_send()
             y_relay(d, q).wait_send()
-        for d in (1, 2, 3):
-            z_copy(d, q).wait_send()
+        z_far(q).wait_send()
+        s_copy(3, q).wait_send()
         l_copy(q).wait_send()
         x_copy(q).wait_send()
 
@@ -599,7 +606,7 @@
             pltpu.VMEM((8192, 1024), BF16),
             pltpu.VMEM((512, 1024), BF16),
             pltpu.VMEM((1024, 2048), BF16),
-            pltpu.VMEM((2, 2, 128, 1024), BF16),
+            pltpu.VMEM((ND, 64, 1024), BF16),
             pltpu.VMEM((19, 128, 1024), BF16),
             pltpu.VMEM((256, 8192), BF16),
             pltpu.VMEM((3, 64, 8192), BF16),
@@ -626,10 +633,12 @@
             dma((3, 12)),
             dma((4, NF)),
             dma((4, NF)),
-            dma((2,)),
             dma((ND,)),
-            dma((3, ND)),
-            dma((3, ND)),
+            dma((4, ND)),
+            dma((4,)),
+            dma((4,)),
+            dma((ND,)),
+            dma((ND,)),
             dma((ND,)),
             dma((ND,)),
             dma((NF,)),

time: 143 us -> 166 us (1.16)
  Pallas kernels: 140 us -> 164 us
    pallas_call x1, Pallas kernels: 137 us -> 161 us  [local(): pl.pallas_call(block_kernel, out_shape=results, in_specs=[hbm] * 6, out_s...]
where the time goes in v6:
time: 166 us
  Pallas kernels  164 us (99%)
    pallas_call x1, Pallas kernels, local(): pl.pallas_call(block_kernel, out_shape=results, in_specs=[hbm] * 6, out_s...  161 us

profile of v6, /device:TPU:0, one launch (start us, length us, event | category | flops | bytes accessed | tf_op | source)
XLA Modules:
  0.0 165.8 jit_solution(12511241274698237468)
XLA Ops:
  0.6 1.3 broadcast_in_dim.3.bias_hbm
  1.9 160.7 %block.1 = (bf16[32,8192]{1,0:T(8,128)(2,1)}, bf16[1024,1024]{1,0:T(8,128)(2,1)}, f32[8,1024]{1,0:T(8,128)}, f32[2,8192]{1,0:T(2,128)}, f32[2,8192]{1,0:T(2,128)}) custom-call(bf16[32,8192]{1,0:T(8,128)(2,1)} %tok_hbm.1, bf16[2,8192]{1,0:T(2,128)(2,1)} %shift_hbm.1, bf16[2,8192]{1,0:T(2,128)(2,1)} %scale_hbm.1, bf16[8192,1024]{1,0:T(8,128)(2,1)} %w_hbm.1, ...), custom_call_target="tpu_custom_call" | custom-call | tf_op jit(solution)/shard_map/block/pallas_call | solution.py:594
  162.6 3.2 %results.1 = (bf16[32,8192]{1,0:T(8,128)(2,1)}, bf16[1024,1024]{1,0:T(8,128)(2,1)}, f32[1,1024]{1,0:T(1,128)}, f32[2,8192]{1,0:T(2,128)}, f32[2,8192]{1,0:T(2,128)}) custom-call(bf16[32,8192]{1,0:T(8,128)(2,1)} %get-tuple-element.15.a, bf16[1024,1024]{1,0:T(8,128)(2,1)} %get-tuple-element.16.b, f32[8,1024]{1,0:T(8,128)} %get-tuple-element.17.c, ...), custom_call_target="tpu_custom_call" | custom-call | tf_op jit(solution)/shard_map/results/pallas_call | solution.py:658

commit v7 on v6

--- a/solution.py
+++ b/solution.py
@@ -62,9 +62,10 @@
 
 SOON = ((0, 0), (0, 1), (3, 0), (1, 0))
 LATE = ((3, 1), (1, 1), (2, 0), (2, 1))
+BLOCKS = (((0, 0), (0, 1)), ((3, 0), (1, 0)), ((3, 1), (1, 1)), ((2, 0), (2, 1)))
+HALVES = (BLOCKS[0] + BLOCKS[1], BLOCKS[2] + BLOCKS[3])
 NF = 8
 ND = 8
-BLOCKS = (((0, 0), (0, 1)), ((3, 0), (1, 0)), ((3, 1), (1, 1)), ((2, 0), (2, 1)))
 
 
 def block_kernel(
@@ -252,53 +253,58 @@
                     y_start(2)
 
     def s_copy(b, j):
-        there = share.at[2 * j + b // 2, pl.ds((b % 2) * 64, 64)]
-        return remote(sb.at[j], there, s_send.at[j], s_recv.at[b, j], sib)
-
-    def z_whole(zz, ll):
-        k = (zz // 2) * 2 + ll
-        there = zr.at[3 - zz, pl.ds(ll * 32, 32)]
-        return remote(zs.at[rows(0, zz, ll)], there, zw_send.at[k], zw_recv.at[k], ring[zz])
+        k = j % 4
+        return remote(sb.at[k], share.at[2 * j + b], s_send.at[k], s_recv.at[b, j], sib)
+
+    def z_whole(zz):
+        k = zz // 2
+        there = zr.at[3 - zz, pl.ds(0, 32)]
+        return remote(zs.at[rows(0, zz, 0)], there, zw_send.at[k], zw_recv.at[k], ring[zz])
+
+    def z_near(zz, j):
+        k, t = zz // 2, cols(j, dc)
+        there = zr.at[3 - zz, pl.ds(32, 32), t]
+        return remote(zs.at[rows(0, zz, 1), t], there, z_send.at[k, j], z_recv.at[k, j], ring[zz])
 
     def z_far(j):
         t = cols(j, dc)
-        return remote(zs.at[pl.ds(128, 64), t], zr.at[1, :, t], z_send.at[j], z_recv.at[j], ring[2])
+        return remote(zs.at[pl.ds(128, 64), t], zr.at[1, :, t], z_send.at[2, j], z_recv.at[2, j], ring[2])
 
     def core_sum(b, j):
         t = cols(j, dc)
-        unit, first_row = 2 * j + b // 2, (b % 2) * 64
-        landed(share.at[unit, pl.ds(first_row, 64)], s_recv.at[b, j])
-        for k, piece in enumerate(BLOCKS[b]):
-            theirs = share[unit, first_row + k * 32 : first_row + k * 32 + 32].astype(F32)
+        landed(share.at[2 * j + b], s_recv.at[b, j])
+        for k, piece in enumerate(HALVES[b]):
+            theirs = share[2 * j + b, k * 32 : k * 32 + 32].astype(F32)
             zs[rows(0, *piece), t] = (zs[rows(0, *piece), t].astype(F32) + theirs).astype(BF16)
-        if b == 3:
+        if b == 1:
+            z_near(3, j).start()
+            z_near(1, j).start()
             z_far(j).start()
 
-    def normed(b):
-        at = [rows(cc, *piece) for cc in (0, 1) for piece in BLOCKS[b]]
-
-        @pl.loop(0, ND)
+    def normed(b, low, high):
+        at = [rows(cc, *piece) for cc in (0, 1) for piece in HALVES[b]]
+
+        @pl.loop(low, high)
         def _(j):
-            if b > 0:
-                s_copy(b - 1, j).wait_send()
-
-            @pl.loop(0, dc // 512)
-            def _(i):
-                t = pl.ds(pl.multiple_of(j * dc + i * 512, 512), 512)
-                x = jnp.concatenate([g[r, :] for r in at], axis=0)
-                p = lax.dot_general(x, w[t, :], (((1,), (1,)), ((), ())), preferred_element_type=F32)
-                p = p.astype(BF16)
-                for k, piece in enumerate(BLOCKS[b]):
-                    zs[rows(0, *piece), t] = p[k * 32 : k * 32 + 32]
-                sb[j, :, cols(i, 512)] = p[64:128]
-
+            @pl.when(4 * b + j >= 4)
+            def _():
+                s_copy(b, j).wait_send()
+
+            t = cols(j, dc)
+            x = jnp.concatenate([g[r, :] for r in at], axis=0)
+            p = lax.dot_general(x, w[t, :], (((1,), (1,)), ((), ())), preferred_element_type=F32)
+            p = p.astype(BF16)
+            for k, piece in enumerate(HALVES[b]):
+                zs[rows(0, *piece), t] = p[k * 32 : k * 32 + 32]
+            sb[j % 4] = p[128:256]
             s_copy(b, j).start()
 
             @pl.when(j >= 1)
             def _():
                 core_sum(b, j - 1)
 
-        core_sum(b, ND - 1)
+        if high == ND:
+            core_sum(b, ND - 1)
 
     own, near_pair = (0, 0, 0), (0, 0, 1)
     send(own, (0, 3, 0), ring[1], (0,))
@@ -343,14 +349,13 @@
     block(BLOCKS[0])
     block(BLOCKS[1])
     ring_piece(1)
-    normed(0)
-    normed(1)
+    normed(0, 0, ND)
     ring_rest(1, "first")
     opposite_piece(0)
     block(BLOCKS[2])
     opposite_piece(1)
-    z_whole(3, 0).start()
-    z_whole(1, 0).start()
+    z_whole(3).start()
+    z_whole(1).start()
     pass_on(SOON, "whole")
     block(BLOCKS[3], last=True)
     own_columns = pltpu.make_async_copy(n.at[:, cols(y, 2048)], cb.at[pl.ds(0, 512)], own_sem)
@@ -396,7 +401,9 @@
 
     def z_sum(j):
         t = cols(j, dc)
-        landed(zr.at[1, :, t], z_recv.at[j])
+        landed(zr.at[1, :, t], z_recv.at[2, j])
+        for zz in (1, 3):
+            landed(zr.at[3 - zz, pl.ds(32, 32), t], z_recv.at[zz // 2, j])
         total = zs[0:64, t].astype(F32)
         for s in range(3):
             total += zr[s, :, t].astype(F32)
@@ -416,12 +423,10 @@
         stats[2] += lane_sums(scaled)
         stats[3] += lane_sums(scaled * hat)
 
-    normed(2)
-    z_whole(3, 1).start()
-    z_whole(1, 1).start()
+    normed(1, 0, 4)
     y_pass(0)
     pass_on(LATE, "first")
-    normed(3)
+    normed(1, 4, ND)
     y_pass(1)
     own_columns.wait()
     for cp in moved:
@@ -442,8 +447,7 @@
         @pl.when(q == 3)
         def _():
             for zz in (1, 3):
-                for ll in (0, 1):
-                    landed(zr.at[3 - zz, pl.ds(ll * 32, 32)], zw_recv.at[(zz // 2) * 2 + ll])
+                landed(zr.at[3 - zz, pl.ds(0, 32)], zw_recv.at[zz // 2])
 
         @pl.when((q >= 3) & (q <= 6))
         def _():
@@ -545,8 +549,9 @@
     for cp in pending + sent + [columns_copy(d, piece, "second") for piece in LATE for d in (1, 2, 3)]:
         cp.wait_send()
     for zz in (1, 3):
-        for ll in (0, 1):
-            z_whole(zz, ll).wait_send()
+        z_whole(zz).wait_send()
+    for j in range(4):
+        s_copy(1, j).wait_send()
 
     @pl.loop(0, NF)
     def _(q):
@@ -554,7 +559,8 @@
             y_copy(d, q).wait_send()
             y_relay(d, q).wait_send()
         z_far(q).wait_send()
-        s_copy(3, q).wait_send()
+        z_near(1, q).wait_send()
+        z_near(3, q).wait_send()
         l_copy(q).wait_send()
         x_copy(q).wait_send()
 
@@ -606,7 +612,7 @@
             pltpu.VMEM((8192, 1024), BF16),
             pltpu.VMEM((512, 1024), BF16),
             pltpu.VMEM((1024, 2048), BF16),
-            pltpu.VMEM((ND, 64, 1024), BF16),
+            pltpu.VMEM((4, 128, 1024), BF16),
             pltpu.VMEM((19, 128, 1024), BF16),
             pltpu.VMEM((256, 8192), BF16),
             pltpu.VMEM((3, 64, 8192), BF16),
@@ -633,12 +639,12 @@
             dma((3, 12)),
             dma((4, NF)),
             dma((4, NF)),
-            dma((ND,)),
-            dma((4, ND)),
             dma((4,)),
-            dma((4,)),
-            dma((ND,)),
-            dma((ND,)),
+            dma((2, ND)),
+            dma((2,)),
+            dma((2,)),
+            dma((3, ND)),
+            dma((3, ND)),
             dma((ND,)),
             dma((ND,)),
             dma((NF,)),

time: 166 us -> 149 us (0.90)
  Pallas kernels: 164 us -> 147 us
    pallas_call x1, Pallas kernels: 161 us -> 144 us  [local(): pl.pallas_call(block_kernel, out_shape=results, in_specs=[hbm] * 6, out_s...]
where the time goes in v7:
time: 149 us
  Pallas kernels  147 us (99%)
    pallas_call x1, Pallas kernels, local(): pl.pallas_call(block_kernel, out_shape=results, in_specs=[hbm] * 6, out_s...  144 us
    pallas_call x1, Pallas kernels, local(): pl.pallas_call(result_kernel, out_shape=tuple(final), in_specs=[hbm] * 5,...  3.2 us

profile of v7, /device:TPU:0, one launch (start us, length us, event | category | flops | bytes accessed | tf_op | source)
XLA Modules:
  0.0 149.1 jit_solution(3461313940539699983)
XLA Ops:
  0.6 1.3 broadcast_in_dim.3.bias_hbm
  1.9 143.8 %block.1 = (bf16[32,8192]{1,0:T(8,128)(2,1)}, bf16[1024,1024]{1,0:T(8,128)(2,1)}, f32[8,1024]{1,0:T(8,128)}, f32[2,8192]{1,0:T(2,128)}, f32[2,8192]{1,0:T(2,128)}) custom-call(bf16[32,8192]{1,0:T(8,128)(2,1)} %tok_hbm.1, bf16[2,8192]{1,0:T(2,128)(2,1)} %shift_hbm.1, bf16[2,8192]{1,0:T(2,128)(2,1)} %scale_hbm.1, bf16[8192,1024]{1,0:T(8,128)(2,1)} %w_hbm.1, ...), custom_call_target="tpu_custom_call" | custom-call | tf_op jit(solution)/shard_map/block/pallas_call | solution.py:600
  145.7 3.2 %results.1 = (bf16[32,8192]{1,0:T(8,128)(2,1)}, bf16[1024,1024]{1,0:T(8,128)(2,1)}, f32[1,1024]{1,0:T(1,128)}, f32[2,8192]{1,0:T(2,128)}, f32[2,8192]{1,0:T(2,128)}) custom-call(bf16[32,8192]{1,0:T(8,128)(2,1)} %get-tuple-element.15.a, bf16[1024,1024]{1,0:T(8,128)(2,1)} %get-tuple-element.16.b, f32[8,1024]{1,0:T(8,128)} %get-tuple-element.17.c, ...), custom_call_target="tpu_custom_call" | custom-call | tf_op jit(solution)/shard_map/results/pallas_call | solution.py:664

commit v8 on v7

--- a/solution.py
+++ b/solution.py
@@ -423,10 +423,9 @@
         stats[2] += lane_sums(scaled)
         stats[3] += lane_sums(scaled * hat)
 
-    normed(1, 0, 4)
+    normed(1, 0, 5)
     y_pass(0)
     pass_on(LATE, "first")
-    normed(1, 4, ND)
     y_pass(1)
     own_columns.wait()
     for cp in moved:
@@ -444,20 +443,28 @@
             y_start(q + 3)
 
     def rows_step(q):
-        @pl.when(q == 3)
+        @pl.when(q == 0)
+        def _():
+            normed(1, 5, ND)
+
+        @pl.when(q == 5)
         def _():
             for zz in (1, 3):
                 landed(zr.at[3 - zz, pl.ds(0, 32)], zw_recv.at[zz // 2])
 
-        @pl.when((q >= 3) & (q <= 6))
-        def _():
-            z_sum(2 * q - 6)
-            z_sum(2 * q - 5)
-
-        @pl.when(q >= 4)
-        def _():
-            row_sum(2 * q - 8)
-            row_sum(2 * q - 7)
+        for k in range(3):
+            j = 3 * (q - 5) + k
+
+            @pl.when((j >= 0) & (j < ND))
+            def _():
+                z_sum(j)
+
+        for k in range(3):
+            j = 3 * (q - 6) + k
+
+            @pl.when(j >= 0)
+            def _():
+                row_sum(j)
 
     @pl.loop(0, 5)
     def _(q):
@@ -492,6 +499,8 @@
         weight_sum(q - 5)
 
 
+    row_sum(ND - 2)
+    row_sum(ND - 1)
     near = (peer()[0], z + 1 - 2 * lax.rem(z, 2), peer()[2])
     hops = [
         remote(term.at[k], trec.at[k], t_send.at[k], t_recv.at[k], to)

time: 149 us -> 157 us (1.054)
  Pallas kernels: 147 us -> 154 us
    pallas_call x1, Pallas kernels: 144 us -> 151 us  [local(): pl.pallas_call(block_kernel, out_shape=results, in_specs=[hbm] * 6, out_s...]
where the time goes in v8:
time: 157 us; the launch traced here: 156 us
  Pallas kernels  154 us (98%)
    pallas_call x1, Pallas kernels, local(): pl.pallas_call(block_kernel, out_shape=results, in_specs=[hbm] * 6, out_s...  151 us
    pallas_call x1, Pallas kernels, local(): pl.pallas_call(result_kernel, out_shape=tuple(final), in_specs=[hbm] * 5,...  3.2 us

profile of v8, /device:TPU:0, one launch (start us, length us, event | category | flops | bytes accessed | tf_op | source)
XLA Modules:
  0.0 156.4 jit_solution(18380528137351370199)
XLA Ops:
  0.6 1.3 broadcast_in_dim.3.bias_hbm
  1.9 151.1 %block.1 = (bf16[32,8192]{1,0:T(8,128)(2,1)}, bf16[1024,1024]{1,0:T(8,128)(2,1)}, f32[8,1024]{1,0:T(8,128)}, f32[2,8192]{1,0:T(2,128)}, f32[2,8192]{1,0:T(2,128)}) custom-call(bf16[32,8192]{1,0:T(8,128)(2,1)} %tok_hbm.1, bf16[2,8192]{1,0:T(2,128)(2,1)} %shift_hbm.1, bf16[2,8192]{1,0:T(2,128)(2,1)} %scale_hbm.1, bf16[8192,1024]{1,0:T(8,128)(2,1)} %w_hbm.1, ...), custom_call_target="tpu_custom_call" | custom-call | tf_op jit(solution)/shard_map/block/pallas_call | solution.py:609
  153.0 3.2 %results.1 = (bf16[32,8192]{1,0:T(8,128)(2,1)}, bf16[1024,1024]{1,0:T(8,128)(2,1)}, f32[1,1024]{1,0:T(1,128)}, f32[2,8192]{1,0:T(2,128)}, f32[2,8192]{1,0:T(2,128)}) custom-call(bf16[32,8192]{1,0:T(8,128)(2,1)} %get-tuple-element.15.a, bf16[1024,1024]{1,0:T(8,128)(2,1)} %get-tuple-element.16.b, f32[8,1024]{1,0:T(8,128)} %get-tuple-element.17.c, ...), custom_call_target="tpu_custom_call" | custom-call | tf_op jit(solution)/shard_map/results/pallas_call | solution.py:673

commit v9 on v5

--- a/solution.py
+++ b/solution.py
@@ -361,7 +361,9 @@
             landed(gt.at[r, pl.ds(1024, 512)], y_recv.at[1 + 2 * half, q])
 
         share[part(q)] = weight_tile(q, (1 - h) * 1024)
-        x_copy(q).start()
+        @pl.when(q < NF - 1)
+        def _():
+            x_copy(q).start()
 
     def weight_second(q):
         share[NF + q] = weight_tile(q, h * 1024)
@@ -479,13 +481,18 @@
         weight_sum(q - 5)
 
     z_sum(ND - 1)
+    x_copy(NF - 1).start()
     row_sum(ND - 2)
     row_sum(ND - 1)
 
     near = (peer()[0], z + 1 - 2 * lax.rem(z, 2), peer()[2])
     hops = [
         remote(term.at[k], trec.at[k], t_send.at[k], t_recv.at[k], to)
-        for k, to in enumerate((sib, pair, near, ring[2]))
+        for k, to in enumerate((sib, near, ring[2]))
+    ]
+    both = [
+        remote(src, dst, t_send.at[k], t_recv.at[k], pair)
+        for src, dst, k in ((term.at[2], trec.at[3], 3), (trec.at[2], term.at[3], 4))
     ]
     hops[0].start()
     nt = (((1,), (1,)), ((), ()))
@@ -514,17 +521,21 @@
     ]
     outs[0].start()
 
-    for k in (1, 2):
-        hops[k].wait_recv()
-        term[k + 1] = term[k] + trec[k]
-        hops[k + 1].start()
-        weight_sum(2 + k)
+    hops[1].wait_recv()
+    term[2] = term[1] + trec[1]
+    hops[2].start()
+    both[0].start()
+    weight_sum(3)
+    hops[2].wait_recv()
+    both[1].start()
+    weight_sum(4)
     b_copy.wait()
     brec[...] = bsum[...] + brec[...]
     outs[1].start()
-    hops[3].wait_recv()
+    for cp in both:
+        cp.wait_recv()
     first = (z < 2).astype(F32) > 0.5
-    near_sum, far_sum = term[3], trec[3]
+    near_sum, far_sum = term[2] + trec[3], trec[2] + term[3]
     shift_grad[0:1, :] = jnp.where(first, near_sum[0:1], far_sum[0:1])
     shift_grad[1:2, :] = jnp.where(first, far_sum[0:1], near_sum[0:1])
     scale_grad[0:1, :] = jnp.where(first, near_sum[1:2], far_sum[1:2])
@@ -534,8 +545,8 @@
     for q in (5, 6, 7):
         weight_sum(q)
 
-    for k in range(4):
-        hops[k].wait_send()
+    for cp in hops + both:
+        cp.wait_send()
     for cp in pending + sent + [columns_copy(d, piece, "second") for piece in LATE for d in (1, 2, 3)]:
         cp.wait_send()
     s_copy(0).wait_send()
@@ -636,8 +647,8 @@
             dma((NF,)),
             dma((1,)),
             dma((1,)),
-            dma((4,)),
-            dma((4,)),
+            dma((5,)),
+            dma((5,)),
         ],
         compiler_params=pltpu.CompilerParams(
             collective_id=0, has_side_effects=True, vmem_limit_bytes=61 * MIB

time: 143 us -> 140 us (0.979)
  Pallas kernels: 140 us -> 138 us
    pallas_call x1, Pallas kernels: 137 us -> 135 us  [local(): pl.pallas_call(block_kernel, out_shape=results, in_specs=[hbm] * 6, out_s...]
where the time goes in v9:
time: 140 us
  Pallas kernels  138 us (99%)
    pallas_call x1, Pallas kernels, local(): pl.pallas_call(block_kernel, out_shape=results, in_specs=[hbm] * 6, out_s...  135 us
    pallas_call x1, Pallas kernels, local(): pl.pallas_call(result_kernel, out_shape=tuple(final), in_specs=[hbm] * 5,...  3.2 us

profile of v9, /device:TPU:0, one launch (start us, length us, event | category | flops | bytes accessed | tf_op | source)
XLA Modules:
  0.0 139.9 jit_solution(11416814982694856861)
XLA Ops:
  0.6 1.3 broadcast_in_dim.3.bias_hbm
  1.9 134.6 %block.1 = (bf16[32,8192]{1,0:T(8,128)(2,1)}, bf16[1024,1024]{1,0:T(8,128)(2,1)}, f32[8,1024]{1,0:T(8,128)}, f32[2,8192]{1,0:T(2,128)}, f32[2,8192]{1,0:T(2,128)}) custom-call(bf16[32,8192]{1,0:T(8,128)(2,1)} %tok_hbm.1, bf16[2,8192]{1,0:T(2,128)(2,1)} %shift_hbm.1, bf16[2,8192]{1,0:T(2,128)(2,1)} %scale_hbm.1, bf16[8192,1024]{1,0:T(8,128)(2,1)} %w_hbm.1, ...), custom_call_target="tpu_custom_call" | custom-call | tf_op jit(solution)/shard_map/block/pallas_call | solution.py:598
  136.5 3.2 %results.1 = (bf16[32,8192]{1,0:T(8,128)(2,1)}, bf16[1024,1024]{1,0:T(8,128)(2,1)}, f32[1,1024]{1,0:T(1,128)}, f32[2,8192]{1,0:T(2,128)}, f32[2,8192]{1,0:T(2,128)}) custom-call(bf16[32,8192]{1,0:T(8,128)(2,1)} %get-tuple-element.15.a, bf16[1024,1024]{1,0:T(8,128)(2,1)} %get-tuple-element.16.b, f32[8,1024]{1,0:T(8,128)} %get-tuple-element.17.c, ...), custom_call_target="tpu_custom_call" | custom-call | tf_op jit(solution)/shard_map/results/pallas_call | solution.py:660
